TPU v7x, 32 devices: a whole 2x2x4 slice. The times are simulated.
32 devices in a mesh: member: 4 (over z), tile: 8 (over y, x, core).
Axes of the slice: x: 2, y: 2, z: 4, core: 2. Of those that a mesh axis runs over, the one named last changes fastest.
Arguments:
- adjoint_final: bfloat16 [4, 32, 256, 192], P('member', None, 'tile'), may hold values from -6 to 6
- states: bfloat16 [2, 4, 32, 256, 192], P(None, 'member', None, 'tile'), may hold values from -12 to 12
- kernel: float32 [7, 7, 192], replicated, may hold values from -0.875 to 0.875
- norm_gain: float32 [192], replicated, may hold values from 0.1 to 1.9
- up_weight: bfloat16 [192, 768], replicated, may hold values from -0.4375 to 0.4375
- up_bias: float32 [768], replicated, may hold values from -4 to 4
- down_weight: bfloat16 [768, 192], replicated, may hold values from -0.21875 to 0.21875
- obs_cell: int32 [2, 8, 8, 16], P(None, 'tile'), may hold values from 0 to 127
- obs_count: int32 [2, 8, 8], P(None, 'tile'), may hold values from 1 to 16, 64 in all within a row
- obs_value: bfloat16 [2, 8, 8, 16, 192], P(None, 'tile'), may hold values from -6 to 6
- obs_error: bfloat16 [2, 8, 8, 16], P(None, 'tile'), may hold values from 0.099609375 to 1
Outputs:
- adjoint_initial: bfloat16 [4, 32, 256, 192], P('member', None, 'tile')
Inputs may be any that keep to these rules, and one draw needn't show every extreme that they name: `obs_cell`: a cell number is latitude offset within the band times 32 plus longitude offset within the tile. `obs_count`: the counts of one band and time add up to 64, and the largest of them is 16.
All inputs are finite; a program needn't handle non-finite values.
Results may differ from a plain program's by a relative error of at most 0.006.
Values may be sent and summed in bfloat16 or wider, within the bound.
A program may use at most 64 MiB of HBM per device.

v0:
```python
import math

import jax
import jax.numpy as jnp
from jax import lax
from jax.sharding import PartitionSpec as P

slope_coef = math.sqrt(2.0 / math.pi)
cubic_coef = 0.044715
norm_eps = 1e-06


def extended(array, sides, width):
    for axis, dim in sides:
        peers, length = (lax.axis_size(axis), array.shape[dim])
        up = [(i, (i + 1) % peers) for i in range(peers)]
        down = [(j, i) for i, j in up]
        last = lax.slice_in_dim(array, length - width, length, axis=dim)
        initial = lax.slice_in_dim(array, 0, width, axis=dim)
        before = lax.ppermute(last, axis, up)
        after = lax.ppermute(initial, axis, down)
        array = jnp.concatenate([before, array, after], axis=dim)
    return array


def gelu_slope(preact):
    inner_arg = slope_coef * (preact + cubic_coef * preact * preact * preact)
    tanh_val = jnp.tanh(inner_arg)
    return 0.5 * (1.0 + tanh_val) + 0.5 * preact * (1.0 - tanh_val * tanh_val) * slope_coef * (
        1.0 + 3.0 * cubic_coef * preact * preact
    )


def wrap_edges(field_in):
    return extended(field_in, (("tile", 1),), 3)


def pad_rows(field_in):
    return jnp.pad(field_in, ((3, 3), (0, 0), (0, 0)))


def depthwise(padded, kernel, lat_count, lon_width):
    summed = jnp.zeros((lat_count, lon_width, padded.shape[2]), jnp.float32)
    for row_tap in range(7):
        for col_tap in range(7):
            summed = (
                summed
                + kernel[row_tap, col_tap]
                * padded[row_tap : row_tap + lat_count, col_tap : col_tap + lon_width]
            )
    return summed


def depthwise_adjoint(padded, kernel, lat_count, lon_width):
    summed = jnp.zeros((lat_count, lon_width, padded.shape[2]), jnp.float32)
    for row_tap in range(7):
        for col_tap in range(7):
            summed = (
                summed
                + kernel[row_tap, col_tap]
                * padded[
                    6 - row_tap : 6 - row_tap + lat_count, 6 - col_tap : 6 - col_tap + lon_width
                ]
            )
    return summed


def departures(sampled_raw, values, errors, live_mask):
    members = lax.axis_size("member")
    sampled = sampled_raw.astype(jnp.float32)
    summed, squares = lax.psum((sampled, sampled * sampled), "member")
    ens_mean = summed / members
    ens_var = squares / members - ens_mean * ens_mean
    ratio = (sampled - values.astype(jnp.float32)) / (
        errors.astype(jnp.float32)[..., None] + ens_var
    )
    return jnp.where(live_mask[..., None], ratio, 0.0).astype(jnp.bfloat16)


def local_index(band_cells, lon_width, band_rows):
    band_ids = jnp.arange(band_cells.shape[0], dtype=jnp.int32)[:, None]
    return (band_ids * band_rows + band_cells // lon_width) * lon_width + band_cells % lon_width


def scatter_rows(row_vals, flat_index, cell_total, channels):
    target = jnp.zeros((cell_total, channels), jnp.float32)
    return target.at[flat_index.reshape(-1)].add(row_vals.reshape(-1, channels).astype(jnp.float32))


def obs_forcing(state_now, cell_ids, counts, values, errors):
    lat_count, lon_width, channels = state_now.shape
    tile_count = lax.axis_size("tile")
    band_rows = lat_count // tile_count
    slot_count = cell_ids.shape[1]
    banded = lax.all_to_all(state_now, "tile", split_axis=0, concat_axis=1, tiled=True)
    tile_ids = jnp.arange(tile_count, dtype=jnp.int32)[:, None]
    band_index = (
        cell_ids // lon_width * (tile_count * lon_width)
        + tile_ids * lon_width
        + cell_ids % lon_width
    )
    sampled = banded.reshape(-1, channels)[band_index]
    live_mask = jnp.arange(slot_count, dtype=jnp.int32)[None, :] < counts[:, None]
    dep_rows = departures(sampled, values, errors, live_mask)
    got_rows, got_cells = (
        lax.all_to_all(dep_rows, "tile", split_axis=0, concat_axis=0, tiled=True),
        lax.all_to_all(cell_ids, "tile", split_axis=0, concat_axis=0, tiled=True),
    )
    forcing = scatter_rows(
        got_rows, local_index(got_cells, lon_width, band_rows), lat_count * lon_width, channels
    )
    return forcing.reshape(lat_count, lon_width, channels)


def member_step(adjoint, state, forcing, kernel, norm_gain, up_weight, up_bias, down_weight):
    lat_count, lon_width, channels = state.shape
    hidden = depthwise(
        pad_rows(wrap_edges(state).astype(jnp.float32)), kernel, lat_count, lon_width
    )
    centred = hidden - jnp.mean(hidden, axis=-1, keepdims=True)
    inv_std = lax.rsqrt(jnp.mean(centred * centred, axis=-1, keepdims=True) + norm_eps)
    unit_norm = centred * inv_std
    normed = (unit_norm * norm_gain).astype(jnp.bfloat16)
    preact = (
        jnp.dot(normed.reshape(-1, channels), up_weight, preferred_element_type=jnp.float32)
        + up_bias
    )
    adj_act = lax.dot_general(
        adjoint.reshape(-1, channels),
        down_weight,
        (((1,), (1,)), ((), ())),
        preferred_element_type=jnp.float32,
    )
    adj_pre = (adj_act * gelu_slope(preact)).astype(jnp.bfloat16)
    adj_norm = lax.dot_general(
        adj_pre, up_weight, (((1,), (1,)), ((), ())), preferred_element_type=jnp.float32
    ).reshape(state.shape)
    scaled = adj_norm * norm_gain
    adj_hidden = (
        inv_std
        * (
            scaled
            - jnp.mean(scaled, axis=-1, keepdims=True)
            - unit_norm * jnp.mean(scaled * unit_norm, axis=-1, keepdims=True)
        )
    ).astype(jnp.bfloat16)
    spread_back = depthwise_adjoint(
        pad_rows(wrap_edges(adj_hidden).astype(jnp.float32)), kernel, lat_count, lon_width
    )
    return (adjoint.astype(jnp.float32) + spread_back + forcing).astype(jnp.bfloat16)


def per_device(
    adjoint_final,
    states,
    kernel,
    norm_gain,
    up_weight,
    up_bias,
    down_weight,
    obs_cell,
    obs_count,
    obs_value,
    obs_error,
):
    adjoint = adjoint_final[0]
    for section_idx in range(states.shape[0]):
        state_now = states[section_idx, 0]
        forcing = obs_forcing(
            state_now,
            obs_cell[section_idx, 0],
            obs_count[section_idx, 0],
            obs_value[section_idx, 0],
            obs_error[section_idx, 0],
        )
        adjoint = member_step(
            adjoint, state_now, forcing, kernel, norm_gain, up_weight, up_bias, down_weight
        )
    return adjoint[None]


def solution(mesh):
    placed = (
        P("member", None, "tile", None),
        P(None, "member", None, "tile", None),
        P(),
        P(),
        P(),
        P(),
        P(),
        P(None, "tile", None, None),
        P(None, "tile", None),
        P(None, "tile", None, None, None),
        P(None, "tile", None, None),
    )
    return jax.shard_map(
        per_device,
        mesh=mesh,
        in_specs=placed,
        out_specs=P("member", None, "tile", None),
        check_vma=False,
    )
```

profile of v0, /device:TPU:1, one launch (start us, length us, event | category | flops | bytes accessed | tf_op | source)
XLA Modules:
  0.0 196.9 jit_solution(18071029776396864418)
XLA Ops:
  6.5 2.3 %slice_bitcast_fusion.1 = (bf16[32,32,192]{2,1,0:T(8,128)(2,1)}, bf16[32,32,192]{2,1,0:T(8,128)(2,1)}) fusion(bf16[2,1,32,32,192]{4,3,2,1,0:T(8,128)(2,1)} %param.12), kind=kLoop, calls=%fused_computation.605 | loop fusion | bytes 1572864 | tf_op jit(solution)/shard_map/squeeze | solution.py:168
  8.9 1.0 fusion.427
  9.9 2.7 %collective-permute-start = (bf16[32,3,192]{2,1,0:T(4,128)(2,1)S(1)}, bf16[32,3,192]{2,1,0:T(4,128)(2,1)S(1)}, u32[]{:S(2)}, u32[]{:S(2)}) collective-permute-start(bf16[32,3,192]{2,1,0:T(4,128)(2,1)S(1)} %get-tuple-element.19), channel_id=1, source_target_pairs={{0,1},{1,2},{2,3},{3,4},{4,5},{5,6},{6,7},{7,0},{8,9},{9,10},{10,1... | collective-permute-start | bytes 110600 | tf_op jit(solution)/shard_map/ppermute | solution.py:20
  12.5 1.0 fusion.428
  13.6 1.8 collective-permute-start.4
  15.4 1.3 fusion.432
  16.7 5.2 %all-to-all-start = ((s32[8,1,16]{2,1,0:T(1,128)}), s32[8,1,16]{2,1,0:T(1,128)S(1)}, u32[]{:S(2)}, u32[]{:S(2)}) async-start(s32[8,1,16]{2,1,0:T(1,128)} %bitcast.55), calls=%async_computation | async-start | bytes 8192 | tf_op jit(solution)/shard_map/all_to_all | solution.py:107
  21.9 1.0 fusion.429
  23.0 1.0 fusion.430
  24.2 0.9 fusion.431
  27.4 1.3 bitcast_convert_fusion.1
  28.7 2.2 %fusion.433 = f32[1024,768]{1,0:T(8,128)} fusion(bf16[1024,192]{1,0:T(8,128)(2,1)S(1)} %bitcast.169, bf16[768,192]{0,1:T(8,128)(2,1)S(1)} %copy-done), kind=kOutput, calls=%fused_computation.705 | convolution fusion | flops 301989888 | bytes 3833856 | tf_op jit(solution)/shard_map/dot_general | solution.py:128
  32.2 4.2 %all-to-all-start.3 = ((s32[8,1,16]{2,1,0:T(1,128)}), s32[8,1,16]{2,1,0:T(1,128)S(1)}, u32[]{:S(2)}, u32[]{:S(2)}) async-start(s32[8,1,16]{2,1,0:T(1,128)} %bitcast.73), calls=%async_computation.3 | async-start | bytes 8192 | tf_op jit(solution)/shard_map/all_to_all | solution.py:107
  37.8 2.5 %all-to-all-done.3 = s32[8,1,16]{2,1,0:T(1,128)S(1)} async-done(((s32[8,1,16]{2,1,0:T(1,128)}), s32[8,1,16]{2,1,0:T(1,128)S(1)}, u32[]{:S(2)}, u32[]{:S(2)}) %all-to-all-start.3) | async-done | bytes 544 | tf_op jit(solution)/shard_map/all_to_all | solution.py:107
  40.3 4.1 %all-to-all-start.1 = ((bf16[32,32,192]{2,1,0:T(8,128)(2,1)}), bf16[32,32,192]{2,1,0:T(8,128)(2,1)S(1)}, u32[]{:S(2)}, u32[]{:S(2)}) async-start(bf16[32,32,192]{2,1,0:T(8,128)(2,1)} %get-tuple-element.13), calls=%async_computation.1 | async-start | bytes 1048576 | tf_op jit(solution)/shard_map/all_to_all | solution.py:95
  45.8 1.3 maximum_convert_fusion
  47.4 8.5 %fusion.423 = (f32[32,32]{1,0:T(8,128)S(1)}, f32[32,32,192]{2,1,0:T(8,128)}) fusion(f32[192]{0:T(256)S(1)} %bitcast.371, f32[192]{0:T(256)S(1)} %bitcast.375, f32[192]{0:T(256)S(1)} %bitcast.187, f32[192]{0:T(256)S(1)} %bitcast.191, f32[192]{0:T(256)S(1)} %bitcast.195, f32[192]{0:T(256)S(1)} %bitcast.199, f32[192]{0:T(256)S(1)} %bitcast.203, ...), kind=kLoop, calls=%fused_computation.696 | loop fusion | flops 19266560 | bytes 9491456 | tf_op jit(solution)/shard_map/reduce_sum | solution.py:120
  56.0 1.3 maximum_convert_fusion.2
  57.3 9.1 %fusion.421 = (f32[32,32]{1,0:T(8,128)S(1)}, f32[32,32,192]{2,1,0:T(8,128)S(1)}) fusion(f32[192]{0:T(256)} %bitcast.372, f32[192]{0:T(256)} %bitcast.376, f32[192]{0:T(256)S(1)} %bitcast.188, f32[192]{0:T(256)S(1)} %bitcast.192, f32[192]{0:T(256)S(1)} %bitcast.196, f32[192]{0:T(256)S(1)} %bitcast.200, f32[192]{0:T(256)S(1)} %bitcast.204, ...), kind=kLoop, calls=%fused_computation.695 | loop fusion | flops 19266560 | bytes 9481984 | tf_op jit(solution)/shard_map/reduce_sum | solution.py:120
  66.4 1.6 multiply_reduce_fusion.3
  68.4 2.4 %multiply_convert_fusion.3 = bf16[32,32,192]{2,1,0:T(8,128)(2,1)} fusion(f32[32,32,192]{2,1,0:T(8,128)} %get-tuple-element.12, f32[192]{0:T(256)S(1)} %copy-done.9, f32[32,32]{1,0:T(8,128)S(1)} %get-tuple-element.91, f32[32,32]{1,0:T(8,128)S(1)} %broadcast_multiply_fusion.3), kind=kLoop, calls=%fused_computation.590 | loop fusion | flops 786432 | bytes 1188608 | tf_op jit(solution)/shard_map/convert_element_type | solution.py:123
  70.8 5.7 %multiply_reduce_fusion.5 = (f32[1024]{0:T(1024)S(1)}, f32[1024,192]{0,1:T(8,128)}) fusion(f32[192]{0:T(256)S(1)} %copy-done.9, bf16[192,768]{1,0:T(8,128)(2,1)} %param.15, f32[1024,768]{1,0:T(8,128)} %fusion.433, bf16[1024,192]{1,0:T(8,128)(2,1)} %bitcast.180, f32[768]{0:T(1024)S(1)} %copy-done.99), kind=kOutput, calls=%fused_computation.595 | convolution fusion | flops 620100608 | bytes 4628224 | tf_op jit(solution)/shard_map/dot_general | solution.py:135
  76.5 2.4 %copy.20 = f32[1024,192]{1,0:T(8,128)} copy(f32[1024,192]{0,1:T(8,128)} %get-tuple-element.87) | data formatting | bytes 1572864 | tf_op jit(solution)/shard_map/dot_general | solution.py:135
  78.9 1.7 multiply_reduce_fusion.2
  80.7 4.2 %all-to-all-start.4 = ((bf16[32,32,192]{2,1,0:T(8,128)(2,1)}), bf16[32,32,192]{2,1,0:T(8,128)(2,1)}, u32[]{:S(2)}, u32[]{:S(2)}) async-start(bf16[32,32,192]{2,1,0:T(8,128)(2,1)} %get-tuple-element.14), calls=%async_computation.4 | async-start | bytes 1048576 | tf_op jit(solution)/shard_map/all_to_all | solution.py:95
  85.1 2.8 %multiply_convert_fusion.1 = (bf16[32,32,192]{2,1,0:T(8,128)(2,1)}, bf16[32,32,192]{2,1,0:T(8,128)(2,1)S(1)}) fusion(f32[32,32,192]{2,1,0:T(8,128)S(1)} %get-tuple-element.10, f32[32,32]{1,0:T(8,128)S(1)} %get-tuple-element.90, f32[32,32]{1,0:T(8,128)S(1)} %broadcast_multiply_fusion.1, f32[192]{0:T(256)S(1)} %copy-done.9, ...), kind=kLoop, calls=%fused_computation.585 | loop fusion | flops 2359296 | bytes 3171072 | tf_op jit(solution)/shard_map/convert_element_type | solution.py:123
  88.0 3.8 %all-to-all-done.4 = bf16[32,32,192]{2,1,0:T(8,128)(2,1)} async-done(((bf16[32,32,192]{2,1,0:T(8,128)(2,1)}), bf16[32,32,192]{2,1,0:T(8,128)(2,1)}, u32[]{:S(2)}, u32[]{:S(2)}) %all-to-all-start.4) | async-done | bytes 393248 | tf_op jit(solution)/shard_map/all_to_all | solution.py:95
  91.8 1.1 copy.25
  93.1 0.8 gather_fusion
  94.0 0.8 gather_fusion.1
  95.6 3.2 %collective-permute-start.2 = (bf16[32,3,192]{2,1,0:T(4,128)(2,1)S(1)}, bf16[32,3,192]{2,1,0:T(4,128)(2,1)S(1)}, u32[]{:S(2)}, u32[]{:S(2)}) collective-permute-start(bf16[32,3,192]{2,1,0:T(4,128)(2,1)S(1)} %get-tuple-element.17), channel_id=1, source_target_pairs={{0,1},{1,2},{2,3},{3,4},{4,5},{5,6},{6,7},{7,0},{8,9},{9,10},{10,1... | collective-permute-start | bytes 110600 | tf_op jit(solution)/shard_map/ppermute | solution.py:20
  98.9 21.0 %all-reduce.10 = (f32[8,16,192]{2,1,0:T(8,128)S(1)}, f32[8,16,192]{2,1,0:T(8,128)S(1)}) all-reduce(bf16[8,16,192]{2,1,0:T(8,128)(2,1)S(1)} %bitcast.177, bf16[8,16,192]{2,1,0:T(8,128)(2,1)S(1)} %bitcast.174), channel_id=1, replica_groups=mesh['member'=4,'tile'=8] {'member'}, use_global_device_ids=true, to_apply=%region_12.13 | all-reduce | flops 49152 | bytes 294912 | tf_op jit(solution)/shard_map/psum | solution.py:71
  119.9 13.8 %all-reduce.9.cloned.1.call-done = (f32[8,16,192]{2,1,0:T(8,128)}, f32[8,16,192]{2,1,0:T(8,128)}) async-done(((f32[8,16,192]{2,1,0:T(8,128)}, f32[8,16,192]{2,1,0:T(8,128)}), (f32[8,16,192]{2,1,0:T(8,128)}, f32[8,16,192]{2,1,0:T(8,128)})) %all-reduce.9.cloned.1.call-update) | async-done | bytes 196624 | tf_op jit(solution)/shard_map/psum | solution.py:71
  133.7 1.8 fusion.390
  135.5 5.8 %all-to-all-start.2 = ((bf16[8,16,192]{2,1,0:T(8,128)(2,1)}), bf16[8,16,192]{2,1,0:T(8,128)(2,1)S(1)}, u32[]{:S(2)}, u32[]{:S(2)}) async-start(bf16[8,16,192]{2,1,0:T(8,128)(2,1)} %get-tuple-element.23), calls=%async_computation.2 | async-start | bytes 131072 | tf_op jit(solution)/shard_map/all_to_all | solution.py:106
  141.3 1.3 maximum_convert_fusion.1
  142.6 2.8 %all-to-all-done.2 = bf16[8,16,192]{2,1,0:T(8,128)(2,1)S(1)} async-done(((bf16[8,16,192]{2,1,0:T(8,128)(2,1)}), bf16[8,16,192]{2,1,0:T(8,128)(2,1)S(1)}, u32[]{:S(2)}, u32[]{:S(2)}) %all-to-all-start.2) | async-done | bytes 49184 | tf_op jit(solution)/shard_map/all_to_all | solution.py:106
  145.5 4.1 %all-to-all-start.5 = ((bf16[8,16,192]{2,1,0:T(8,128)(2,1)}), bf16[8,16,192]{2,1,0:T(8,128)(2,1)S(1)}, u32[]{:S(2)}, u32[]{:S(2)}) async-start(bf16[8,16,192]{2,1,0:T(8,128)(2,1)} %get-tuple-element.24), calls=%async_computation.5 | async-start | bytes 131072 | tf_op jit(solution)/shard_map/all_to_all | solution.py:106
  149.6 2.4 %scatter_custom_fusion = f32[1024,192]{1,0:T(8,128)} fusion(s32[128]{0:T(128)} %get-tuple-element.84, f32[]{:T(128)} %constant.90.clone.1, bf16[128,192]{1,0:T(8,128)(2,1)S(1)} %bitcast.182), kind=kCustom, calls=%fused_computation.603 | custom fusion | flops 49152 | bytes 836096 | tf_op jit(solution)/shard_map/scatter-add | solution.py:87
  152.2 10.1 %add_convert_fusion.1 = bf16[32,32,192]{2,1,0:T(8,128)(2,1)S(1)} fusion(f32[32,32,192]{2,1,0:T(8,128)} %bitcast.168, f32[32,38,192]{2,1,0:T(8,128)S(1)} %maximum_convert_fusion.1, bf16[1,32,32,192]{3,2,1,0:T(8,128)(2,1)} %param.11, f32[192]{0:T(256)} %bitcast.373, f32[192]{0:T(256)} %bitcast.377, f32[192]{0:T(256)S(1)} %bitcast.189, f32[192]{0:T(256)S(1)} %bitcast.193, ...), kind=kLoop, calls=%fused_computation.587 | loop fusion | flops 19857408 | bytes 10270208 | tf_op jit(solution)/shard_map/convert_element_type | solution.py:150
  162.3 2.2 %fusion.434 = f32[1024,768]{1,0:T(8,128)} fusion(bf16[1024,192]{1,0:T(8,128)(2,1)S(1)} %bitcast.166, bf16[768,192]{0,1:T(8,128)(2,1)S(1)} %copy-done), kind=kOutput, calls=%fused_computation.706 | convolution fusion | flops 301989888 | bytes 3833856 | tf_op jit(solution)/shard_map/dot_general | solution.py:128
  164.5 5.4 %multiply_reduce_fusion.4 = (f32[1024]{0:T(1024)S(1)}, f32[1024,192]{0,1:T(8,128)}) fusion(f32[192]{0:T(256)S(1)} %copy-done.9, bf16[192,768]{1,0:T(8,128)(2,1)S(1)} %copy-done.98, f32[1024,768]{1,0:T(8,128)} %fusion.434, bf16[1024,192]{1,0:T(8,128)(2,1)S(1)} %bitcast.179, f32[768]{0:T(1024)S(1)} %copy-done.100), kind=kOutput, calls=%fused_computation.594 | convolution fusion | flops 620100608 | bytes 4628224 | tf_op jit(solution)/shard_map/dot_general | solution.py:135
  169.8 1.5 copy.23
  173.7 1.7 collective-permute-start.6
  175.4 1.9 scatter_custom_fusion.1
  177.3 1.8 collective-permute-done.7
  179.1 1.3 maximum_convert_fusion.3
  180.6 9.5 %fusion.382 = bf16[1,32,32,192]{3,2,1,0:T(8,128)(2,1)} fusion(f32[32,32,192]{2,1,0:T(8,128)S(1)} %bitcast.167, f32[32,38,192]{2,1,0:T(8,128)S(1)} %maximum_convert_fusion.3, f32[192]{0:T(256)S(1)} %bitcast.374, f32[192]{0:T(256)S(1)} %bitcast.378, f32[192]{0:T(256)S(1)} %bitcast.190, f32[192]{0:T(256)S(1)} %bitcast.194, f32[192]{0:T(256)S(1)} %bitcast.198, ...), kind=kLoop, calls=%fused_computation.606 | loop fusion | flops 19857408 | bytes 10667008 | tf_op jit(solution)/shard_map/broadcast_in_dim | solution.py:179
  (251 shorter events, 10.2 us)
Async XLA Ops:
  9.9 35.9 %collective-permute-start = (bf16[32,3,192]{2,1,0:T(4,128)(2,1)S(1)}, bf16[32,3,192]{2,1,0:T(4,128)(2,1)S(1)}, u32[]{:S(2)}, u32[]{:S(2)}) collective-permute-start(bf16[32,3,192]{2,1,0:T(4,128)(2,1)S(1)} %get-tuple-element.19), channel_id=1, source_target_pairs={{0,1},{1,2},{2,3},{3,4},{4,5},{5,6},{6,7},{7,0},{8,9},{9,10},{10,1... | collective-permute-start | bytes 110600 | tf_op jit(solution)/shard_map/ppermute | solution.py:20
  12.5 33.2 %collective-permute-start.1 = (bf16[32,3,192]{2,1,0:T(4,128)(2,1)S(1)}, bf16[32,3,192]{2,1,0:T(4,128)(2,1)S(1)}, u32[]{:S(2)}, u32[]{:S(2)}) collective-permute-start(bf16[32,3,192]{2,1,0:T(4,128)(2,1)S(1)} %get-tuple-element.20), channel_id=1, source_target_pairs={{1,0},{2,1},{3,2},{4,3},{5,4},{6,5},{7,6},{0,7},{9,8},{10,9},{11,1... | collective-permute-start | bytes 110600 | tf_op jit(solution)/shard_map/ppermute | solution.py:21
  13.6 42.4 %collective-permute-start.4 = (bf16[32,3,192]{2,1,0:T(4,128)(2,1)S(1)}, bf16[32,3,192]{2,1,0:T(4,128)(2,1)S(1)}, u32[]{:S(2)}, u32[]{:S(2)}) collective-permute-start(bf16[32,3,192]{2,1,0:T(4,128)(2,1)S(1)} %get-tuple-element.21), channel_id=1, source_target_pairs={{0,1},{1,2},{2,3},{3,4},{4,5},{5,6},{6,7},{7,0},{8,9},{9,10},{10,1... | collective-permute-start | bytes 110600 | tf_op jit(solution)/shard_map/ppermute | solution.py:20
  15.4 40.6 %collective-permute-start.5 = (bf16[32,3,192]{2,1,0:T(4,128)(2,1)S(1)}, bf16[32,3,192]{2,1,0:T(4,128)(2,1)}, u32[]{:S(2)}, u32[]{:S(2)}) collective-permute-start(bf16[32,3,192]{2,1,0:T(4,128)(2,1)S(1)} %get-tuple-element.22), channel_id=1, source_target_pairs={{1,0},{2,1},{3,2},{4,3},{5,4},{6,5},{7,6},{0,7},{9,8},{10,9},{11,1... | collective-permute-start | bytes 110600 | tf_op jit(solution)/shard_map/ppermute | solution.py:21
  16.7 15.5 %all-to-all-start = ((s32[8,1,16]{2,1,0:T(1,128)}), s32[8,1,16]{2,1,0:T(1,128)S(1)}, u32[]{:S(2)}, u32[]{:S(2)}) async-start(s32[8,1,16]{2,1,0:T(1,128)} %bitcast.55), calls=%async_computation | async-start | bytes 8192 | tf_op jit(solution)/shard_map/all_to_all | solution.py:107
  22.9 24.2 %copy-start.10 = (f32[1,1,192]{2,1,0:T(1,128)}, f32[1,1,192]{2,1,0:T(1,128)S(1)}, u32[]{:S(2)}) copy-start(f32[1,1,192]{2,1,0:T(1,128)S(1)} %get-tuple-element.37) | copy-start | bytes 2308
  22.9 24.2 %copy-start.12 = (f32[1,1,192]{2,1,0:T(1,128)}, f32[1,1,192]{2,1,0:T(1,128)S(1)}, u32[]{:S(2)}) copy-start(f32[1,1,192]{2,1,0:T(1,128)S(1)} %get-tuple-element.38) | copy-start | bytes 2308
  22.9 24.2 %copy-start.14 = (f32[1,1,192]{2,1,0:T(1,128)}, f32[1,1,192]{2,1,0:T(1,128)S(1)}, u32[]{:S(2)}) copy-start(f32[1,1,192]{2,1,0:T(1,128)S(1)} %get-tuple-element.39) | copy-start | bytes 2308
  22.9 24.2 %copy-start.16 = (f32[1,1,192]{2,1,0:T(1,128)}, f32[1,1,192]{2,1,0:T(1,128)S(1)}, u32[]{:S(2)}) copy-start(f32[1,1,192]{2,1,0:T(1,128)S(1)} %get-tuple-element.40) | copy-start | bytes 2308
  32.2 8.2 %all-to-all-start.3 = ((s32[8,1,16]{2,1,0:T(1,128)}), s32[8,1,16]{2,1,0:T(1,128)S(1)}, u32[]{:S(2)}, u32[]{:S(2)}) async-start(s32[8,1,16]{2,1,0:T(1,128)} %bitcast.73), calls=%async_computation.3 | async-start | bytes 8192 | tf_op jit(solution)/shard_map/all_to_all | solution.py:107
  40.3 40.3 %all-to-all-start.1 = ((bf16[32,32,192]{2,1,0:T(8,128)(2,1)}), bf16[32,32,192]{2,1,0:T(8,128)(2,1)S(1)}, u32[]{:S(2)}, u32[]{:S(2)}) async-start(bf16[32,32,192]{2,1,0:T(8,128)(2,1)} %get-tuple-element.13), calls=%async_computation.1 | async-start | bytes 1048576 | tf_op jit(solution)/shard_map/all_to_all | solution.py:95
  80.7 11.1 %all-to-all-start.4 = ((bf16[32,32,192]{2,1,0:T(8,128)(2,1)}), bf16[32,32,192]{2,1,0:T(8,128)(2,1)}, u32[]{:S(2)}, u32[]{:S(2)}) async-start(bf16[32,32,192]{2,1,0:T(8,128)(2,1)} %get-tuple-element.14), calls=%async_computation.4 | async-start | bytes 1048576 | tf_op jit(solution)/shard_map/all_to_all | solution.py:95
  84.9 48.8 %all-reduce.9.cloned.1.call-start = ((), (), s32[]{:S(2)}) async-start(), calls=%async_computation.6 | async-start | bytes 524288 | tf_op jit(solution)/shard_map/psum | solution.py:71
  87.9 53.4 %copy-start.2 = (bf16[32,32,192]{2,1,0:T(8,128)(2,1)}, bf16[32,32,192]{2,1,0:T(8,128)(2,1)S(1)}, u32[]{:S(2)}) copy-start(bf16[32,32,192]{2,1,0:T(8,128)(2,1)S(1)} %get-tuple-element.81) | copy-start | bytes 1179652
  87.9 45.8 %copy-start.8 = (bf16[2,1,8,16,192]{4,3,2,1,0:T(8,128)(2,1)S(1)}, bf16[2,1,8,16,192]{4,3,2,1,0:T(8,128)(2,1)}, u32[]{:S(2)}) copy-start(bf16[2,1,8,16,192]{4,3,2,1,0:T(8,128)(2,1)} %param.20) | copy-start | bytes 294916
  87.9 45.8 %copy-start.92 = (f32[8,16]{1,0:T(8,128)S(1)}, f32[8,16]{1,0:T(8,128)}, u32[]{:S(2)}) copy-start(f32[8,16]{1,0:T(8,128)} %get-tuple-element.78) | copy-start | bytes 1540
  87.9 45.8 %copy-start.93 = (f32[8,16]{1,0:T(8,128)S(1)}, f32[8,16]{1,0:T(8,128)}, u32[]{:S(2)}) copy-start(f32[8,16]{1,0:T(8,128)} %get-tuple-element.79) | copy-start | bytes 1540
  87.9 45.8 %copy-start.96 = (pred[8,16]{1,0:T(8,128)(4,1)S(1)}, pred[8,16]{1,0:T(8,128)(4,1)}, u32[]{:S(2)}) copy-start(pred[8,16]{1,0:T(8,128)(4,1)} %get-tuple-element.94) | copy-start | bytes 388
  87.9 45.8 %copy-start.97 = (pred[8,16]{1,0:T(8,128)(4,1)S(1)}, pred[8,16]{1,0:T(8,128)(4,1)}, u32[]{:S(2)}) copy-start(pred[8,16]{1,0:T(8,128)(4,1)} %get-tuple-element.95) | copy-start | bytes 388
  92.9 59.1 %copy-start.11 = (f32[1,1,192]{2,1,0:T(1,128)S(1)}, f32[1,1,192]{2,1,0:T(1,128)}, u32[]{:S(2)}) copy-start(f32[1,1,192]{2,1,0:T(1,128)} %copy-done.10) | copy-start | bytes 2308
  92.9 59.1 %copy-start.13 = (f32[1,1,192]{2,1,0:T(1,128)S(1)}, f32[1,1,192]{2,1,0:T(1,128)}, u32[]{:S(2)}) copy-start(f32[1,1,192]{2,1,0:T(1,128)} %copy-done.12) | copy-start | bytes 2308
  92.9 59.1 %copy-start.15 = (f32[1,1,192]{2,1,0:T(1,128)S(1)}, f32[1,1,192]{2,1,0:T(1,128)}, u32[]{:S(2)}) copy-start(f32[1,1,192]{2,1,0:T(1,128)} %copy-done.14) | copy-start | bytes 2308
  92.9 59.1 %copy-start.17 = (f32[1,1,192]{2,1,0:T(1,128)S(1)}, f32[1,1,192]{2,1,0:T(1,128)}, u32[]{:S(2)}) copy-start(f32[1,1,192]{2,1,0:T(1,128)} %copy-done.16) | copy-start | bytes 2308
  92.9 59.1 %copy-start.19 = (f32[1,1,192]{2,1,0:T(1,128)S(1)}, f32[1,1,192]{2,1,0:T(1,128)}, u32[]{:S(2)}) copy-start(f32[1,1,192]{2,1,0:T(1,128)} %copy-done.18) | copy-start | bytes 2308
  92.9 59.1 %copy-start.21 = (f32[1,1,192]{2,1,0:T(1,128)S(1)}, f32[1,1,192]{2,1,0:T(1,128)}, u32[]{:S(2)}) copy-start(f32[1,1,192]{2,1,0:T(1,128)} %copy-done.20) | copy-start | bytes 2308
  92.9 59.1 %copy-start.23 = (f32[1,1,192]{2,1,0:T(1,128)S(1)}, f32[1,1,192]{2,1,0:T(1,128)}, u32[]{:S(2)}) copy-start(f32[1,1,192]{2,1,0:T(1,128)} %copy-done.22) | copy-start | bytes 2308
  92.9 59.1 %copy-start.25 = (f32[1,1,192]{2,1,0:T(1,128)S(1)}, f32[1,1,192]{2,1,0:T(1,128)}, u32[]{:S(2)}) copy-start(f32[1,1,192]{2,1,0:T(1,128)} %copy-done.24) | copy-start | bytes 2308
  92.9 59.1 %copy-start.27 = (f32[1,1,192]{2,1,0:T(1,128)S(1)}, f32[1,1,192]{2,1,0:T(1,128)}, u32[]{:S(2)}) copy-start(f32[1,1,192]{2,1,0:T(1,128)} %copy-done.26) | copy-start | bytes 2308
  93.0 59.1 %copy-start.29 = (f32[1,1,192]{2,1,0:T(1,128)S(1)}, f32[1,1,192]{2,1,0:T(1,128)}, u32[]{:S(2)}) copy-start(f32[1,1,192]{2,1,0:T(1,128)} %copy-done.28) | copy-start | bytes 2308
  93.0 59.1 %copy-start.31 = (f32[1,1,192]{2,1,0:T(1,128)S(1)}, f32[1,1,192]{2,1,0:T(1,128)}, u32[]{:S(2)}) copy-start(f32[1,1,192]{2,1,0:T(1,128)} %copy-done.30) | copy-start | bytes 2308
  93.0 59.1 %copy-start.33 = (f32[1,1,192]{2,1,0:T(1,128)S(1)}, f32[1,1,192]{2,1,0:T(1,128)}, u32[]{:S(2)}) copy-start(f32[1,1,192]{2,1,0:T(1,128)} %copy-done.32) | copy-start | bytes 2308
  93.0 59.1 %copy-start.35 = (f32[1,1,192]{2,1,0:T(1,128)S(1)}, f32[1,1,192]{2,1,0:T(1,128)}, u32[]{:S(2)}) copy-start(f32[1,1,192]{2,1,0:T(1,128)} %copy-done.34) | copy-start | bytes 2308
  93.0 59.1 %copy-start.37 = (f32[1,1,192]{2,1,0:T(1,128)S(1)}, f32[1,1,192]{2,1,0:T(1,128)}, u32[]{:S(2)}) copy-start(f32[1,1,192]{2,1,0:T(1,128)} %copy-done.36) | copy-start | bytes 2308
  93.0 59.1 %copy-start.39 = (f32[1,1,192]{2,1,0:T(1,128)S(1)}, f32[1,1,192]{2,1,0:T(1,128)}, u32[]{:S(2)}) copy-start(f32[1,1,192]{2,1,0:T(1,128)} %copy-done.38) | copy-start | bytes 2308
  93.0 59.1 %copy-start.41 = (f32[1,1,192]{2,1,0:T(1,128)S(1)}, f32[1,1,192]{2,1,0:T(1,128)}, u32[]{:S(2)}) copy-start(f32[1,1,192]{2,1,0:T(1,128)} %copy-done.40) | copy-start | bytes 2308
  93.0 59.1 %copy-start.44 = (f32[1,1,192]{2,1,0:T(1,128)S(1)}, f32[1,1,192]{2,1,0:T(1,128)}, u32[]{:S(2)}) copy-start(f32[1,1,192]{2,1,0:T(1,128)} %copy-done.43) | copy-start | bytes 2308
  93.0 59.1 %copy-start.47 = (f32[1,1,192]{2,1,0:T(1,128)S(1)}, f32[1,1,192]{2,1,0:T(1,128)}, u32[]{:S(2)}) copy-start(f32[1,1,192]{2,1,0:T(1,128)} %copy-done.46) | copy-start | bytes 2308
  93.0 59.1 %copy-start.50 = (f32[1,1,192]{2,1,0:T(1,128)S(1)}, f32[1,1,192]{2,1,0:T(1,128)}, u32[]{:S(2)}) copy-start(f32[1,1,192]{2,1,0:T(1,128)} %copy-done.49) | copy-start | bytes 2308
  93.1 59.1 %copy-start.53 = (f32[1,1,192]{2,1,0:T(1,128)S(1)}, f32[1,1,192]{2,1,0:T(1,128)}, u32[]{:S(2)}) copy-start(f32[1,1,192]{2,1,0:T(1,128)} %copy-done.52) | copy-start | bytes 2308
  93.1 59.1 %copy-start.56 = (f32[1,1,192]{2,1,0:T(1,128)S(1)}, f32[1,1,192]{2,1,0:T(1,128)}, u32[]{:S(2)}) copy-start(f32[1,1,192]{2,1,0:T(1,128)} %copy-done.55) | copy-start | bytes 2308
  93.1 59.1 %copy-start.59 = (f32[1,1,192]{2,1,0:T(1,128)S(1)}, f32[1,1,192]{2,1,0:T(1,128)}, u32[]{:S(2)}) copy-start(f32[1,1,192]{2,1,0:T(1,128)} %copy-done.58) | copy-start | bytes 2308
  93.1 59.1 %copy-start.62 = (f32[1,1,192]{2,1,0:T(1,128)S(1)}, f32[1,1,192]{2,1,0:T(1,128)}, u32[]{:S(2)}) copy-start(f32[1,1,192]{2,1,0:T(1,128)} %copy-done.61) | copy-start | bytes 2308
  95.6 45.7 %collective-permute-start.2 = (bf16[32,3,192]{2,1,0:T(4,128)(2,1)S(1)}, bf16[32,3,192]{2,1,0:T(4,128)(2,1)S(1)}, u32[]{:S(2)}, u32[]{:S(2)}) collective-permute-start(bf16[32,3,192]{2,1,0:T(4,128)(2,1)S(1)} %get-tuple-element.17), channel_id=1, source_target_pairs={{0,1},{1,2},{2,3},{3,4},{4,5},{5,6},{6,7},{7,0},{8,9},{9,10},{10,1... | collective-permute-start | bytes 110600 | tf_op jit(solution)/shard_map/ppermute | solution.py:20
  98.9 42.5 %collective-permute-start.3 = (bf16[32,3,192]{2,1,0:T(4,128)(2,1)S(1)}, bf16[32,3,192]{2,1,0:T(4,128)(2,1)S(1)}, u32[]{:S(2)}, u32[]{:S(2)}) collective-permute-start(bf16[32,3,192]{2,1,0:T(4,128)(2,1)S(1)} %get-tuple-element.18), channel_id=1, source_target_pairs={{1,0},{2,1},{3,2},{4,3},{5,4},{6,5},{7,6},{0,7},{9,8},{10,9},{11,1... | collective-permute-start | bytes 110600 | tf_op jit(solution)/shard_map/ppermute | solution.py:21
  135.5 10.0 %all-to-all-start.2 = ((bf16[8,16,192]{2,1,0:T(8,128)(2,1)}), bf16[8,16,192]{2,1,0:T(8,128)(2,1)S(1)}, u32[]{:S(2)}, u32[]{:S(2)}) async-start(bf16[8,16,192]{2,1,0:T(8,128)(2,1)} %get-tuple-element.23), calls=%async_computation.2 | async-start | bytes 131072 | tf_op jit(solution)/shard_map/all_to_all | solution.py:106
  145.5 29.9 %all-to-all-start.5 = ((bf16[8,16,192]{2,1,0:T(8,128)(2,1)}), bf16[8,16,192]{2,1,0:T(8,128)(2,1)S(1)}, u32[]{:S(2)}, u32[]{:S(2)}) async-start(bf16[8,16,192]{2,1,0:T(8,128)(2,1)} %get-tuple-element.24), calls=%async_computation.5 | async-start | bytes 131072 | tf_op jit(solution)/shard_map/all_to_all | solution.py:106
  173.7 3.6 %collective-permute-start.6 = (bf16[32,3,192]{2,1,0:T(4,128)(2,1)S(1)}, bf16[32,3,192]{2,1,0:T(4,128)(2,1)S(1)}, u32[]{:S(2)}, u32[]{:S(2)}) collective-permute-start(bf16[32,3,192]{2,1,0:T(4,128)(2,1)S(1)} %get-tuple-element.15), channel_id=1, source_target_pairs={{0,1},{1,2},{2,3},{3,4},{4,5},{5,6},{6,7},{7,0},{8,9},{9,10},{10,1... | collective-permute-start | bytes 110600 | tf_op jit(solution)/shard_map/ppermute | solution.py:20
  175.4 3.7 %collective-permute-start.7 = (bf16[32,3,192]{2,1,0:T(4,128)(2,1)S(1)}, bf16[32,3,192]{2,1,0:T(4,128)(2,1)S(1)}, u32[]{:S(2)}, u32[]{:S(2)}) collective-permute-start(bf16[32,3,192]{2,1,0:T(4,128)(2,1)S(1)} %get-tuple-element.16), channel_id=1, source_target_pairs={{1,0},{2,1},{3,2},{4,3},{5,4},{6,5},{7,6},{0,7},{9,8},{10,9},{11,1... | collective-permute-start | bytes 110600 | tf_op jit(solution)/shard_map/ppermute | solution.py:21
  (68 other events, 1044.4 us)
Sparse Core Ops, SparseCore 0:
  95.7 38.0 all-reduce.8
where the time goes:
time: 198 us; the launch traced here: 197 us
  other arithmetic  65 us (33%)
  starting transfers between devices  37.2 us (19%)
  waiting for transfers between devices  24.8 us (13%)
  blocking collectives  21 us (11%)
  local copies, waits for them, and re-layouts  18.5 us (9%)
  matrix products  15.5 us (8%)
  between operations  15.1 us (8%)
    psum x1, blocking collectives, departures(): summed, squares = lax.psum((sampled, sampled * sampled), 'member')  21 us
    reduce_sum x2, other arithmetic, member_step(): centred = hidden - jnp.mean(hidden, axis=-1, keepdims=True)  17.6 us
    psum x1, waiting for transfers between devices, departures(): summed, squares = lax.psum((sampled, sampled * sampled), 'member')  13.8 us
    dot_general x2, matrix products, member_step(): lax.dot_general(adj_pre, up_weight, (((1,), (1,)), ((), ())), preferred_e...  11 us
    convert_element_type x1, other arithmetic, member_step(): (adjoint.astype(jnp.float32) + spread_back + forcing).astype(jnp.bfloat16)  10.1 us
    all_to_all x2, starting transfers between devices, obs_forcing(): lax.all_to_all(dep_rows, 'tile', split_axis=0, concat_axis=0, tiled=True)  9.92 us
    broadcast_in_dim x1, other arithmetic, per_device(): return adjoint[None]  9.5 us
    all_to_all x2, starting transfers between devices, obs_forcing(): lax.all_to_all(cell_ids, 'tile', split_axis=0, concat_axis=0, tiled=True)  9.43 us
  transfers between devices with their start and end apart: 15, of which 5 were waited for; matrix products, arithmetic and copies ran while one was open for 41% of the time, Pallas kernels for 0%

commit v1 on v0

v1 whole, which is shorter than its diff:
```python
import functools
import math

import jax
import jax.numpy as jnp
from jax import lax
from jax.experimental import pallas as pl
from jax.experimental.pallas import tpu as pltpu
from jax.sharding import PartitionSpec as P

slope_coef = math.sqrt(2.0 / math.pi)
cubic_coef = 0.044715
norm_eps = 1e-06
MESH = pl.DeviceIdType.MESH
F32, BF16 = jnp.float32, jnp.bfloat16
GROUP = 4
PAD = 8


def gelu_slope(u):
    u2 = u * u
    w = jnp.tanh(u * (slope_coef + (slope_coef * cubic_coef) * u2))
    outer = u * (0.5 * slope_coef + (1.5 * slope_coef * cubic_coef) * u2)
    return (0.5 + 0.5 * w) + (1.0 - w * w) * outer


def kernel(
    tiles, members, adj_ref, st_ref, kern_ref, gain_ref, up_ref, bias_ref, down_ref, pack_ref, out_ref,
    xb, ahb, cur, plane0, plane1, kbr, hbuf, turn, upt, downt, orecv, samp, dep,
    obs_send, obs_recv, mem_send, mem_recv, halo_send, halo_recv,
):
    steps, lat, lon, chan = st_ref.shape
    half, cells, slots = lon // 2, lat * lon, tiles * pack_ref.shape[2]
    rest = chan - 128
    pitch = turn.shape[1] // lon
    rows = GROUP * lat
    t, m = lax.axis_index("tile"), lax.axis_index("member")

    barrier = pltpu.get_barrier_semaphore()
    for d in range(1, tiles):
        pl.semaphore_signal(barrier, inc=1, device_id={"tile": lax.rem(t + d, tiles)}, device_id_type=MESH)
    for d in range(1, members):
        pl.semaphore_signal(barrier, inc=1, device_id={"member": lax.rem(m + d, members)}, device_id_type=MESH)

    def to_lon_major(load, store):
        for i in range(lat):
            v = load(i).astype(F32)
            turn[0, pl.ds(i * pitch, lon), :] = v[:, :128]
            turn[1, pl.ds(i * pitch, lon), :rest] = v[:, 128:]
        for k in range(lon):
            a = turn[0, pl.ds(k, lat, stride=pitch), :]
            b = turn[1, pl.ds(k, lat, stride=pitch), :]
            store(k, a, b[:, :rest])

    def halo_copies(buf, s, n):
        right, left = lax.rem(t + 1, tiles), lax.rem(t + tiles - 1, tiles)
        out = []
        for d, (src, dst, to) in enumerate(((lon, 0, right), (3, lon + 3, left))):
            out.append(pltpu.make_async_remote_copy(
                src_ref=buf.at[s, pl.ds(src, 3)], dst_ref=buf.at[s, pl.ds(dst, 3)],
                send_sem=halo_send.at[n, d], recv_sem=halo_recv.at[n, d],
                device_id={"tile": to}, device_id_type=MESH))
        return out

    for s in range(steps):
        def store_x(k, a, b, s=s):
            xb[s, 3 + k, :, :128] = a.astype(BF16)
            xb[s, 3 + k, :, 128:] = b.astype(BF16)
        to_lon_major(lambda i, s=s: st_ref[s, i], store_x)

    pl.semaphore_wait(barrier, tiles - 1 + members - 1)
    obs = []
    for d in range(1, tiles):
        to = lax.rem(t + d, tiles)
        obs.append(pltpu.make_async_remote_copy(
            src_ref=pack_ref.at[to], dst_ref=orecv.at[t], send_sem=obs_send.at[d], recv_sem=obs_recv.at[d],
            device_id={"tile": to}, device_id_type=MESH))
        obs[-1].start()
    halos = [halo_copies(xb, s, s) for s in range(steps)]
    for pair in halos:
        for c in pair:
            c.start()
    orecv[pl.ds(t, 1)] = pack_ref[pl.ds(t, 1)]

    def store_adj(k, a, b):
        cur[k, :, :128] = a.astype(BF16)
        cur[k, :, 128:] = b.astype(BF16)
    to_lon_major(lambda i: adj_ref[i], store_adj)
    upt[...] = up_ref[...].T
    downt[...] = down_ref[...].T
    for n in range(49):
        kbr[0, n] = jnp.broadcast_to(kern_ref[n:n + 1, :128], (8, 128))
        tail = jnp.broadcast_to(kern_ref[n:n + 1, 128:], (8, rest))
        kbr[1, n, :, :rest] = tail
        kbr[1, n, :, rest:] = tail
    for plane in (plane0, plane1):
        plane[:, :PAD] = jnp.zeros((plane.shape[0], PAD, 128), F32)
        plane[:, PAD + lat:] = jnp.zeros((plane.shape[0], PAD, 128), F32)

    for c in obs:
        c.wait()

    def places(s):
        meta = orecv[:, s, :, 128:].astype(F32).reshape(slots, 128)
        lon_at, lat_at = meta[:, rest:rest + 1], meta[:, rest + 1:rest + 2]
        return meta, lon_at * lat + lat_at

    for s in range(steps):
        _, place = places(s)
        ids = lax.broadcasted_iota(jnp.int32, (slots, cells), 1).astype(F32)
        pick = jnp.where(ids == place, 1.0, 0.0).astype(BF16)
        got = jnp.dot(pick, xb[s, 3:3 + lon].reshape(cells, chan), preferred_element_type=F32)
        samp[pl.ds(m, 1), s] = got.astype(BF16).reshape(1, slots, chan)
    mem = []
    for d in range(1, members):
        mem.append(pltpu.make_async_remote_copy(
            src_ref=samp.at[m], dst_ref=samp.at[m], send_sem=mem_send.at[d], recv_sem=mem_recv.at[d],
            device_id={"member": lax.rem(m + d, members)}, device_id_type=MESH))
        mem[-1].start()

    def build(buf, s, wait):
        def put0(i, _):
            plane0[i, PAD:PAD + lat, :] = buf[s, i, :, :128].astype(F32)
            return 0

        def put1(i, _):
            plane1[i, PAD:PAD + lat, :] = jnp.concatenate(
                [buf[s, i, :, 128:].astype(F32), buf[s, i + half, :, 128:].astype(F32)], axis=-1)
            return 0
        lax.fori_loop(3, lon + 3, put0, 0)
        lax.fori_loop(3, half + 3, put1, 0)
        wait()
        for lo in (0, lon + 3):
            lax.fori_loop(lo, lo + 3, put0, 0)
        for lo in (0, half + 3):
            lax.fori_loop(lo, lo + 3, put1, 0)

    def conv_group(plane, p_id, first, flip):
        acc = [None] * GROUP
        for p in range(7):
            for r in range(GROUP + 6):
                v = plane[first + r, pl.ds(PAD - 3 + p, lat), :].reshape(lat // 8, 8, 128)
                for q in range(7):
                    o = r - q
                    if 0 <= o < GROUP:
                        n = (6 - p) * 7 + (6 - q) if flip else p * 7 + q
                        term = kbr[p_id, n][None] * v
                        acc[o] = term if acc[o] is None else acc[o] + term
        return jnp.concatenate([a.reshape(lat, 128) for a in acc], axis=0)

    def conv(i0, flip):
        hbuf[:rows, :128] = conv_group(plane0, 0, i0, flip)
        hbuf[rows:, :128] = conv_group(plane0, 0, half + i0, flip)
        both = conv_group(plane1, 1, i0, flip)
        hbuf[:rows, 128:] = both[:, :rest]
        hbuf[rows:, 128:] = both[:, rest:]
        return hbuf[...]

    def current(i0):
        return jnp.concatenate(
            [cur[pl.ds(i0, GROUP)].reshape(rows, chan), cur[pl.ds(half + i0, GROUP)].reshape(rows, chan)], axis=0)

    blocks = half // GROUP
    for s in range(steps):
        def wait_x(s=s):
            for c in halos[s]:
                c.wait()
        build(xb, s, wait_x)
        back = halo_copies(ahb, s, steps + s)

        def point(k, _, s=s, back=back):
            i0 = lax.rem(k * (blocks - 1), blocks) * GROUP
            hidden = conv(i0, False)
            centred = hidden - jnp.mean(hidden, axis=-1, keepdims=True)
            inv_std = lax.rsqrt(jnp.mean(centred * centred, axis=-1, keepdims=True) + norm_eps)
            unit = centred * inv_std
            normed = (unit * gain_ref[...]).astype(BF16)
            pre = jnp.dot(normed, up_ref[...], preferred_element_type=F32) + bias_ref[...]
            act = jnp.dot(current(i0), downt[...], preferred_element_type=F32)
            adj_pre = (act * gelu_slope(pre)).astype(BF16)
            scaled = jnp.dot(adj_pre, upt[...], preferred_element_type=F32) * gain_ref[...]
            ah = inv_std * (
                scaled - jnp.mean(scaled, axis=-1, keepdims=True)
                - unit * jnp.mean(scaled * unit, axis=-1, keepdims=True))
            ah = ah.astype(BF16)
            ahb[s, pl.ds(3 + i0, GROUP)] = ah[:rows].reshape(GROUP, lat, chan)
            ahb[s, pl.ds(3 + half + i0, GROUP)] = ah[rows:].reshape(GROUP, lat, chan)

            @pl.when(k == 1)
            def _():
                for c in back:
                    c.start()
            return 0
        lax.fori_loop(0, blocks, point, 0)

        if s == 0:
            for c in mem:
                c.wait()
            for z in range(steps):
                meta, _ = places(z)
                total = squares = None
                for i in range(members):
                    v = samp[i, z].astype(F32)
                    total = v if total is None else total + v
                    squares = v * v if squares is None else squares + v * v
                mean = total / members
                var = squares / members - mean * mean
                own = samp[pl.ds(m, 1), z].astype(F32).reshape(slots, chan)
                value = orecv[:, z, :, :chan].astype(F32).reshape(slots, chan)
                ratio = (own - value) / (meta[:, rest + 2:rest + 3] + var)
                dep[z] = jnp.where(meta[:, rest + 3:rest + 4] > 0.5, ratio, 0.0).astype(BF16)

        def wait_back(back=back):
            for c in back:
                c.wait()
        build(ahb, s, wait_back)
        _, place = places(s)
        line = jnp.broadcast_to(place, (slots, 128)).T[0:1, :]

        def spread(k, _, s=s, line=line):
            i0 = k * GROUP
            back_out = conv(i0, True)
            row = lax.broadcasted_iota(jnp.int32, (2 * rows, slots), 0)
            row = jnp.where(row < rows, row, row + (half * lat - rows)) + i0 * lat
            hit = jnp.where(row.astype(F32) == line, 1.0, 0.0).astype(BF16)
            forcing = jnp.dot(hit, dep[s], preferred_element_type=F32)
            new = current(i0).astype(F32) + back_out + forcing
            if s < steps - 1:
                new = new.astype(BF16)
                cur[pl.ds(i0, GROUP)] = new[:rows].reshape(GROUP, lat, chan)
                cur[pl.ds(half + i0, GROUP)] = new[rows:].reshape(GROUP, lat, chan)
            else:
                for g in range(2 * GROUP):
                    at = (i0 + (g // GROUP) * half + g % GROUP) * pitch
                    part = new[g * lat:(g + 1) * lat]
                    turn[0, pl.ds(at, lat), :] = part[:, :128]
                    turn[1, pl.ds(at, lat), :rest] = part[:, 128:]
            return 0
        lax.fori_loop(0, blocks, spread, 0)

    for i in range(lat):
        out_ref[i, :, :128] = turn[0, pl.ds(i, lon, stride=pitch), :].astype(BF16)
        out_ref[i, :, 128:] = turn[1, pl.ds(i, lon, stride=pitch), :][:, :rest].astype(BF16)


def per_device(
    adjoint_final, states, kernel_w, norm_gain, up_weight, up_bias, down_weight,
    obs_cell, obs_count, obs_value, obs_error,
):
    tiles, members = lax.axis_size("tile"), lax.axis_size("member")
    steps, _, lat, lon, chan = states.shape
    hid, cap = up_weight.shape[1], obs_cell.shape[3]
    band = lat // tiles
    cell = obs_cell[:, 0]
    slot = jnp.arange(cap, dtype=jnp.int32)
    meta = jnp.stack([
        (cell % lon).astype(BF16),
        (cell // lon + lax.axis_index("tile") * band).astype(BF16),
        obs_error[:, 0],
        (slot < obs_count[:, 0][..., None]).astype(BF16)], axis=-1)
    pack = jnp.concatenate([obs_value[:, 0], jnp.pad(meta, ((0, 0),) * 3 + ((0, 256 - chan - 4),))], axis=-1)
    pack = jnp.swapaxes(pack, 0, 1)
    slots = tiles * cap
    pitch = lat + 1
    vm = pl.BlockSpec(memory_space=pltpu.VMEM)
    out = pl.pallas_call(
        functools.partial(kernel, tiles, members),
        out_shape=jax.ShapeDtypeStruct((lat, lon, chan), BF16),
        in_specs=[vm] * 8,
        out_specs=vm,
        scratch_shapes=[
            pltpu.VMEM((steps, lon + 6, lat, chan), BF16),
            pltpu.VMEM((steps, lon + 6, lat, chan), BF16),
            pltpu.VMEM((lon, lat, chan), BF16),
            pltpu.VMEM((lon + 6, lat + 2 * PAD, 128), F32),
            pltpu.VMEM((lon // 2 + 6, lat + 2 * PAD, 128), F32),
            pltpu.VMEM((2, 49, 8, 128), F32),
            pltpu.VMEM((2 * GROUP * lat, chan), F32),
            pltpu.VMEM((2, pitch * lon, 128), F32),
            pltpu.VMEM((hid, chan), BF16),
            pltpu.VMEM((chan, hid), BF16),
            pltpu.VMEM((tiles, steps, cap, 256), BF16),
            pltpu.VMEM((members, steps, slots, chan), BF16),
            pltpu.VMEM((steps, slots, chan), BF16),
            pltpu.SemaphoreType.DMA((tiles,)),
            pltpu.SemaphoreType.DMA((tiles,)),
            pltpu.SemaphoreType.DMA((members,)),
            pltpu.SemaphoreType.DMA((members,)),
            pltpu.SemaphoreType.DMA((2 * steps, 2)),
            pltpu.SemaphoreType.DMA((2 * steps, 2)),
        ],
        compiler_params=pltpu.CompilerParams(
            collective_id=0, has_side_effects=True, vmem_limit_bytes=48 * 1024 * 1024),
    )(
        adjoint_final[0], states[:, 0], kernel_w.reshape(49, chan), norm_gain.reshape(1, chan),
        up_weight, up_bias.reshape(1, hid), down_weight, pack,
    )
    return out[None]


def solution(mesh):
    placed = (
        P("member", None, "tile", None),
        P(None, "member", None, "tile", None),
        P(), P(), P(), P(), P(),
        P(None, "tile", None, None),
        P(None, "tile", None),
        P(None, "tile", None, None, None),
        P(None, "tile", None, None),
    )
    return jax.shard_map(
        per_device, mesh=mesh, in_specs=placed, out_specs=P("member", None, "tile", None), check_vma=False)
```

time: 198 us -> 47.5 us (0.24)
  the two profiles are of different devices: /device:TPU:1 before, /device:TPU:9 now
where the time goes in v1:
time: 47.5 us; the launch traced here: 47.3 us
  Pallas kernels  41.3 us (87%)
  local copies, waits for them, and re-layouts  5.41 us (11%)
    pallas_call x1, Pallas kernels, per_device(): pl.pallas_call(functools.partial(kernel, tiles, members), out_shape=jax.S...  41.3 us
    unnamed x21, local copies, waits for them, and re-layouts  4.1 us

profile of v1, /device:TPU:9, one launch (start us, length us, event | category | flops | bytes accessed | tf_op | source)
XLA Modules:
  0.0 47.3 jit_solution(12341072797134249630)
XLA Ops:
  0.0 0.0 copy-start.7
  0.0 0.7 %copy-done.7 = f32[768]{0:T(1024)S(1)} copy-done((f32[768]{0:T(1024)S(1)}, f32[768]{0:T(1024)}, u32[]{:S(2)}) %copy-start.7) | copy-done | bytes 3096
  0.7 0.0 copy-start.8
  0.7 0.7 %copy-done.8 = s32[2,1,8]{2,1,0:T(1,128)S(1)} copy-done((s32[2,1,8]{2,1,0:T(1,128)S(1)}, s32[2,1,8]{2,1,0:T(1,128)}, u32[]{:S(2)}) %copy-start.8) | copy-done | bytes 88
  1.4 0.0 copy-start.6
  1.4 0.0 copy-start.5
  1.4 0.1 copy.36
  1.5 0.0 copy-start.4
  1.5 0.9 %reshape.130.kern_ref = f32[49,192]{1,0:T(8,128)S(1)} reshape(f32[7,7,192]{2,1,0:T(8,128)} %param.13) | data formatting | bytes 75264 | tf_op jit(solution)/shard_map/reshape | solution.py:295
  2.3 0.1 fusion.8
  2.4 0.0 copy-done.6
  2.4 0.0 copy-start
  2.4 0.2 copy.37
  2.6 0.0 copy-done.5
  2.6 0.2 copy.32
  2.8 0.1 fusion
  2.9 0.1 fusion.12
  3.1 0.9 %copy.40 = bf16[2,1,8,16,192]{4,3,0,2,1:T(8,128)(2,1)S(1)} copy(bf16[2,1,8,16,192]{4,3,2,1,0:T(8,128)(2,1)} %param.20) | data formatting | bytes 196608 | tf_op args[9]
  4.0 0.0 copy-start.1
  4.0 0.1 maximum_bitcast_fusion.pack_ref
  4.1 0.0 copy-done.4
  4.1 0.0 copy-start.2
  4.1 0.0 copy-start.3
  4.1 0.2 copy.38.down_ref
  4.3 0.0 copy-done
  4.3 0.7 %copy-done.1 = bf16[1,32,32,192]{3,2,1,0:T(8,128)(2,1)S(1)} copy-done((bf16[1,32,32,192]{3,2,1,0:T(8,128)(2,1)S(1)}, bf16[1,32,32,192]{3,2,1,0:T(8,128)(2,1)}, u32[]{:S(2)}) %copy-start.1) | copy-done | bytes 393240
  5.0 0.1 copy-done.2
  5.1 0.0 copy-done.3
  5.1 41.3 %shard_map.109 = bf16[32,32,192]{2,1,0:T(8,128)(2,1)S(1)} custom-call(bf16[32,32,192]{2,1,0:T(8,128)(2,1)S(1)} %bitcast.14, bf16[2,32,32,192]{3,2,1,0:T(8,128)(2,1)S(1)} %bitcast.13, f32[49,192]{1,0:T(8,128)S(1)} %reshape.130.kern_ref, f32[1,192]{1,0:T(1,128)S(1)} %bitcast.15, bf16[192,768]{1,0:T(8,128)(2,1)S(1)} %copy-done.2, ...), custom_call_target="tpu_custom_call" | custom-call | tf_op jit(solution)/shard_map/pallas_call | solution.py:266
  46.5 0.8 %copy.42 = bf16[1,32,32,192]{3,2,1,0:T(8,128)(2,1)} copy(bf16[1,32,32,192]{3,2,1,0:T(8,128)(2,1)S(1)} %bitcast.12) | data formatting | bytes 786432
  (1 shorter events, 0.0 us)
Async XLA Ops:
  0.0 0.7 %copy-start.7 = (f32[768]{0:T(1024)S(1)}, f32[768]{0:T(1024)}, u32[]{:S(2)}) copy-start(f32[768]{0:T(1024)} %param.16) | copy-start | bytes 9220
  0.7 0.7 %copy-start.8 = (s32[2,1,8]{2,1,0:T(1,128)S(1)}, s32[2,1,8]{2,1,0:T(1,128)}, u32[]{:S(2)}) copy-start(s32[2,1,8]{2,1,0:T(1,128)} %param.19) | copy-start | bytes 196
  1.4 1.1 %copy-start.6 = (bf16[2,1,8,16]{3,2,1,0:T(8,128)(2,1)S(1)}, bf16[2,1,8,16]{3,2,1,0:T(8,128)(2,1)}, u32[]{:S(2)}) copy-start(bf16[2,1,8,16]{3,2,1,0:T(8,128)(2,1)} %param.21) | copy-start | bytes 1540
  1.4 1.3 %copy-start.5 = (s32[2,1,8,16]{3,2,1,0:T(8,128)S(1)}, s32[2,1,8,16]{3,2,1,0:T(8,128)}, u32[]{:S(2)}) copy-start(s32[2,1,8,16]{3,2,1,0:T(8,128)} %param.18) | copy-start | bytes 3076
  1.5 2.7 %copy-start.4 = (bf16[768,192]{0,1:T(8,128)(2,1)S(1)}, bf16[768,192]{0,1:T(8,128)(2,1)}, u32[]{:S(2)}) copy-start(bf16[768,192]{0,1:T(8,128)(2,1)} %param.17) | copy-start | bytes 884740
  2.4 1.9 %copy-start = (bf16[2,1,32,32,192]{4,3,2,1,0:T(8,128)(2,1)S(1)}, bf16[2,1,32,32,192]{4,3,2,1,0:T(8,128)(2,1)}, u32[]{:S(2)}) copy-start(bf16[2,1,32,32,192]{4,3,2,1,0:T(8,128)(2,1)} %param.12) | copy-start | bytes 2359300
  4.0 1.0 %copy-start.1 = (bf16[1,32,32,192]{3,2,1,0:T(8,128)(2,1)S(1)}, bf16[1,32,32,192]{3,2,1,0:T(8,128)(2,1)}, u32[]{:S(2)}) copy-start(bf16[1,32,32,192]{3,2,1,0:T(8,128)(2,1)} %param.11) | copy-start | bytes 1179652
  4.1 1.0 %copy-start.2 = (bf16[192,768]{1,0:T(8,128)(2,1)S(1)}, bf16[192,768]{1,0:T(8,128)(2,1)}, u32[]{:S(2)}) copy-start(bf16[192,768]{1,0:T(8,128)(2,1)} %up_ref.1) | copy-start | bytes 884740
  4.1 1.0 %copy-start.3 = (f32[192]{0:T(256)S(1)}, f32[192]{0:T(256)}, u32[]{:S(2)}) copy-start(f32[192]{0:T(256)} %param.14) | copy-start | bytes 2308

commit v2 on v1

--- a/solution.py
+++ b/solution.py
@@ -25,8 +25,9 @@
 
 
 def kernel(
-    tiles, members, adj_ref, st_ref, kern_ref, gain_ref, up_ref, bias_ref, down_ref, pack_ref, out_ref,
-    xb, ahb, cur, plane0, plane1, kbr, hbuf, turn, upt, downt, orecv, samp, dep,
+    tiles, members, adj_hbm, st_hbm, kern_hbm, gain_hbm, up_hbm, bias_hbm, down_hbm, obs_hbm, meta_ref, out_ref,
+    adj_ref, st_ref, kern_ref, gain_ref, up_ref, bias_ref, downt, obs_ref, pack_ref,
+    xb, ahb, cur, plane0, plane1, kbr, hbuf, turn, upt, orecv, samp, dep, local_sem,
     obs_send, obs_recv, mem_send, mem_recv, halo_send, halo_recv,
 ):
     steps, lat, lon, chan = st_ref.shape
@@ -35,6 +36,15 @@
     pitch = turn.shape[1] // lon
     rows = GROUP * lat
     t, m = lax.axis_index("tile"), lax.axis_index("member")
+
+    loads = []
+    for src, dst in (
+        (obs_hbm, obs_ref), *((st_hbm.at[s], st_ref.at[s]) for s in range(steps)), (kern_hbm, kern_ref),
+        (up_hbm, up_ref), (adj_hbm, adj_ref), (down_hbm, downt), (gain_hbm, gain_ref), (bias_hbm, bias_ref),
+    ):
+        loads.append(pltpu.make_async_copy(src, dst, local_sem.at[len(loads)]))
+        loads[-1].start()
+    obs_load, st_loads, other_loads = loads[0], loads[1:1 + steps], loads[1 + steps:]
 
     barrier = pltpu.get_barrier_semaphore()
     for d in range(1, tiles):
@@ -62,11 +72,19 @@
                 device_id={"tile": to}, device_id_type=MESH))
         return out
 
-    for s in range(steps):
-        def store_x(k, a, b, s=s):
+    def turn_state(s):
+        def store_x(k, a, b):
             xb[s, 3 + k, :, :128] = a.astype(BF16)
             xb[s, 3 + k, :, 128:] = b.astype(BF16)
-        to_lon_major(lambda i, s=s: st_ref[s, i], store_x)
+        st_loads[s].wait()
+        to_lon_major(lambda i: st_ref[s, i], store_x)
+
+    obs_load.wait()
+    for s in range(steps):
+        pack_ref[:, s, :, :chan] = obs_ref[s]
+        pack_ref[:, s, :, chan:] = meta_ref[s]
+    orecv[pl.ds(t, 1)] = pack_ref[pl.ds(t, 1)]
+    turn_state(0)
 
     pl.semaphore_wait(barrier, tiles - 1 + members - 1)
     obs = []
@@ -77,20 +95,23 @@
             device_id={"tile": to}, device_id_type=MESH))
         obs[-1].start()
     halos = [halo_copies(xb, s, s) for s in range(steps)]
-    for pair in halos:
-        for c in pair:
+    for s in range(steps):
+        if s > 0:
+            turn_state(s)
+        for c in halos[s]:
             c.start()
-    orecv[pl.ds(t, 1)] = pack_ref[pl.ds(t, 1)]
+    for c in other_loads:
+        c.wait()
 
     def store_adj(k, a, b):
         cur[k, :, :128] = a.astype(BF16)
         cur[k, :, 128:] = b.astype(BF16)
     to_lon_major(lambda i: adj_ref[i], store_adj)
     upt[...] = up_ref[...].T
-    downt[...] = down_ref[...].T
     for n in range(49):
-        kbr[0, n] = jnp.broadcast_to(kern_ref[n:n + 1, :128], (8, 128))
-        tail = jnp.broadcast_to(kern_ref[n:n + 1, 128:], (8, rest))
+        taps = kern_ref[n // 7, n % 7:n % 7 + 1, :]
+        kbr[0, n] = jnp.broadcast_to(taps[:, :128], (8, 128))
+        tail = jnp.broadcast_to(taps[:, 128:], (8, rest))
         kbr[1, n, :, :rest] = tail
         kbr[1, n, :, rest:] = tail
     for plane in (plane0, plane1):
@@ -105,18 +126,19 @@
         lon_at, lat_at = meta[:, rest:rest + 1], meta[:, rest + 1:rest + 2]
         return meta, lon_at * lat + lat_at
 
+    mem = []
     for s in range(steps):
         _, place = places(s)
         ids = lax.broadcasted_iota(jnp.int32, (slots, cells), 1).astype(F32)
         pick = jnp.where(ids == place, 1.0, 0.0).astype(BF16)
         got = jnp.dot(pick, xb[s, 3:3 + lon].reshape(cells, chan), preferred_element_type=F32)
         samp[pl.ds(m, 1), s] = got.astype(BF16).reshape(1, slots, chan)
-    mem = []
-    for d in range(1, members):
-        mem.append(pltpu.make_async_remote_copy(
-            src_ref=samp.at[m], dst_ref=samp.at[m], send_sem=mem_send.at[d], recv_sem=mem_recv.at[d],
-            device_id={"member": lax.rem(m + d, members)}, device_id_type=MESH))
-        mem[-1].start()
+        mem.append([])
+        for d in range(1, members):
+            mem[s].append(pltpu.make_async_remote_copy(
+                src_ref=samp.at[m, s], dst_ref=samp.at[m, s], send_sem=mem_send.at[s, d], recv_sem=mem_recv.at[s, d],
+                device_id={"member": lax.rem(m + d, members)}, device_id_type=MESH))
+            mem[s][-1].start()
 
     def build(buf, s, wait):
         def put0(i, _):
@@ -148,13 +170,15 @@
                         acc[o] = term if acc[o] is None else acc[o] + term
         return jnp.concatenate([a.reshape(lat, 128) for a in acc], axis=0)
 
-    def conv(i0, flip):
-        hbuf[:rows, :128] = conv_group(plane0, 0, i0, flip)
-        hbuf[rows:, :128] = conv_group(plane0, 0, half + i0, flip)
+    def conv(i0, flip, to):
+        hbuf[to, :rows, :128] = conv_group(plane0, 0, i0, flip)
+        hbuf[to, rows:, :128] = conv_group(plane0, 0, half + i0, flip)
         both = conv_group(plane1, 1, i0, flip)
-        hbuf[:rows, 128:] = both[:, :rest]
-        hbuf[rows:, 128:] = both[:, rest:]
-        return hbuf[...]
+        hbuf[to, :rows, 128:] = both[:, :rest]
+        hbuf[to, rows:, 128:] = both[:, rest:]
+
+    def at_turn(k):
+        return lax.rem(k * (blocks - 1), blocks) * GROUP
 
     def current(i0):
         return jnp.concatenate(
@@ -168,14 +192,14 @@
         build(xb, s, wait_x)
         back = halo_copies(ahb, s, steps + s)
 
-        def point(k, _, s=s, back=back):
-            i0 = lax.rem(k * (blocks - 1), blocks) * GROUP
-            hidden = conv(i0, False)
+        def point(k, hidden, s=s):
+            i0 = at_turn(k)
             centred = hidden - jnp.mean(hidden, axis=-1, keepdims=True)
             inv_std = lax.rsqrt(jnp.mean(centred * centred, axis=-1, keepdims=True) + norm_eps)
             unit = centred * inv_std
             normed = (unit * gain_ref[...]).astype(BF16)
-            pre = jnp.dot(normed, up_ref[...], preferred_element_type=F32) + bias_ref[...]
+            bias = jnp.concatenate([bias_ref[n:n + 1] for n in range(bias_ref.shape[0])], axis=-1)
+            pre = jnp.dot(normed, up_ref[...], preferred_element_type=F32) + bias
             act = jnp.dot(current(i0), downt[...], preferred_element_type=F32)
             adj_pre = (act * gelu_slope(pre)).astype(BF16)
             scaled = jnp.dot(adj_pre, upt[...], preferred_element_type=F32) * gain_ref[...]
@@ -186,40 +210,45 @@
             ahb[s, pl.ds(3 + i0, GROUP)] = ah[:rows].reshape(GROUP, lat, chan)
             ahb[s, pl.ds(3 + half + i0, GROUP)] = ah[rows:].reshape(GROUP, lat, chan)
 
+        def both_parts(k, _, back=back, point=point):
+            hidden = hbuf[lax.rem(k, 2)]
+            conv(at_turn(k + 1), False, lax.rem(k + 1, 2))
+            point(k, hidden)
+
             @pl.when(k == 1)
             def _():
                 for c in back:
                     c.start()
             return 0
-        lax.fori_loop(0, blocks, point, 0)
-
-        if s == 0:
-            for c in mem:
-                c.wait()
-            for z in range(steps):
-                meta, _ = places(z)
-                total = squares = None
-                for i in range(members):
-                    v = samp[i, z].astype(F32)
-                    total = v if total is None else total + v
-                    squares = v * v if squares is None else squares + v * v
-                mean = total / members
-                var = squares / members - mean * mean
-                own = samp[pl.ds(m, 1), z].astype(F32).reshape(slots, chan)
-                value = orecv[:, z, :, :chan].astype(F32).reshape(slots, chan)
-                ratio = (own - value) / (meta[:, rest + 2:rest + 3] + var)
-                dep[z] = jnp.where(meta[:, rest + 3:rest + 4] > 0.5, ratio, 0.0).astype(BF16)
+        conv(at_turn(0), False, 0)
+        lax.fori_loop(0, blocks - 1, both_parts, 0)
+        point(blocks - 1, hbuf[(blocks - 1) % 2])
+
+        for c in mem[s]:
+            c.wait()
+        meta, place = places(s)
+        total = squares = None
+        for i in range(members):
+            v = samp[i, s].astype(F32)
+            total = v if total is None else total + v
+            squares = v * v if squares is None else squares + v * v
+        mean = total / members
+        var = squares / members - mean * mean
+        own = samp[pl.ds(m, 1), s].astype(F32).reshape(slots, chan)
+        value = orecv[:, s, :, :chan].astype(F32).reshape(slots, chan)
+        ratio = (own - value) / (meta[:, rest + 2:rest + 3] + var)
+        dep[s] = jnp.where(meta[:, rest + 3:rest + 4] > 0.5, ratio, 0.0).astype(BF16)
 
         def wait_back(back=back):
             for c in back:
                 c.wait()
         build(ahb, s, wait_back)
-        _, place = places(s)
         line = jnp.broadcast_to(place, (slots, 128)).T[0:1, :]
 
         def spread(k, _, s=s, line=line):
             i0 = k * GROUP
-            back_out = conv(i0, True)
+            conv(i0, True, 0)
+            back_out = hbuf[0]
             row = lax.broadcasted_iota(jnp.int32, (2 * rows, slots), 0)
             row = jnp.where(row < rows, row, row + (half * lat - rows)) + i0 * lat
             hit = jnp.where(row.astype(F32) == line, 1.0, 0.0).astype(BF16)
@@ -258,42 +287,50 @@
         (cell // lon + lax.axis_index("tile") * band).astype(BF16),
         obs_error[:, 0],
         (slot < obs_count[:, 0][..., None]).astype(BF16)], axis=-1)
-    pack = jnp.concatenate([obs_value[:, 0], jnp.pad(meta, ((0, 0),) * 3 + ((0, 256 - chan - 4),))], axis=-1)
-    pack = jnp.swapaxes(pack, 0, 1)
+    meta = jnp.pad(meta, ((0, 0),) * 3 + ((0, 256 - chan - 4),))
     slots = tiles * cap
     pitch = lat + 1
     vm = pl.BlockSpec(memory_space=pltpu.VMEM)
     out = pl.pallas_call(
         functools.partial(kernel, tiles, members),
         out_shape=jax.ShapeDtypeStruct((lat, lon, chan), BF16),
-        in_specs=[vm] * 8,
+        in_specs=[pl.BlockSpec(memory_space=pltpu.HBM)] * 8 + [vm],
         out_specs=vm,
         scratch_shapes=[
+            pltpu.VMEM((lat, lon, chan), BF16),
+            pltpu.VMEM((steps, lat, lon, chan), BF16),
+            pltpu.VMEM((7, 7, chan), F32),
+            pltpu.VMEM((1, chan), F32),
+            pltpu.VMEM((chan, hid), BF16),
+            pltpu.VMEM((hid // 128, 128), F32),
+            pltpu.VMEM((chan, hid), BF16),
+            pltpu.VMEM((steps, tiles, cap, chan), BF16),
+            pltpu.VMEM((tiles, steps, cap, 256), BF16),
             pltpu.VMEM((steps, lon + 6, lat, chan), BF16),
             pltpu.VMEM((steps, lon + 6, lat, chan), BF16),
             pltpu.VMEM((lon, lat, chan), BF16),
             pltpu.VMEM((lon + 6, lat + 2 * PAD, 128), F32),
             pltpu.VMEM((lon // 2 + 6, lat + 2 * PAD, 128), F32),
             pltpu.VMEM((2, 49, 8, 128), F32),
-            pltpu.VMEM((2 * GROUP * lat, chan), F32),
+            pltpu.VMEM((2, 2 * GROUP * lat, chan), F32),
             pltpu.VMEM((2, pitch * lon, 128), F32),
             pltpu.VMEM((hid, chan), BF16),
-            pltpu.VMEM((chan, hid), BF16),
             pltpu.VMEM((tiles, steps, cap, 256), BF16),
             pltpu.VMEM((members, steps, slots, chan), BF16),
             pltpu.VMEM((steps, slots, chan), BF16),
+            pltpu.SemaphoreType.DMA((steps + 7,)),
             pltpu.SemaphoreType.DMA((tiles,)),
             pltpu.SemaphoreType.DMA((tiles,)),
-            pltpu.SemaphoreType.DMA((members,)),
-            pltpu.SemaphoreType.DMA((members,)),
+            pltpu.SemaphoreType.DMA((steps, members)),
+            pltpu.SemaphoreType.DMA((steps, members)),
             pltpu.SemaphoreType.DMA((2 * steps, 2)),
             pltpu.SemaphoreType.DMA((2 * steps, 2)),
         ],
         compiler_params=pltpu.CompilerParams(
-            collective_id=0, has_side_effects=True, vmem_limit_bytes=48 * 1024 * 1024),
+            collective_id=0, has_side_effects=True, vmem_limit_bytes=127 * 512 * 1024),
     )(
-        adjoint_final[0], states[:, 0], kernel_w.reshape(49, chan), norm_gain.reshape(1, chan),
-        up_weight, up_bias.reshape(1, hid), down_weight, pack,
+        adjoint_final[0], states[:, 0], kernel_w, norm_gain.reshape(1, chan),
+        up_weight, up_bias.reshape(hid // 128, 128), down_weight.T, obs_value[:, 0], meta,
     )
     return out[None]
 

time: 47.5 us -> 51.6 us (1.086)
  the two profiles are of different devices: /device:TPU:9 before, /device:TPU:1 now
where the time goes in v2:
time: 51.6 us; the launch traced here: 51.3 us
  Pallas kernels  46.3 us (90%)
  local copies, waits for them, and re-layouts  4.01 us (8%)
  other arithmetic  0.98 us (2%)
    pallas_call x1, Pallas kernels, per_device(): pl.pallas_call(functools.partial(kernel, tiles, members), out_shape=jax.S...  46.3 us
    unnamed x7, local copies, waits for them, and re-layouts  3.65 us

profile of v2, /device:TPU:1, one launch (start us, length us, event | category | flops | bytes accessed | tf_op | source)
XLA Modules:
  0.0 51.3 jit_solution(8483794960577633732)
XLA Ops:
  0.0 0.0 copy-start.2
  0.0 0.7 %copy-done.2 = s32[2,1,8]{2,1,0:T(1,128)S(1)} copy-done((s32[2,1,8]{2,1,0:T(1,128)S(1)}, s32[2,1,8]{2,1,0:T(1,128)}, u32[]{:S(2)}) %copy-start.2) | copy-done | bytes 88
  0.7 0.0 copy-start.1
  0.7 0.1 fusion.8
  0.8 0.6 %copy-done.1 = bf16[2,1,8,16]{3,2,1,0:T(8,128)(2,1)S(1)} copy-done((bf16[2,1,8,16]{3,2,1,0:T(8,128)(2,1)S(1)}, bf16[2,1,8,16]{3,2,1,0:T(8,128)(2,1)}, u32[]{:S(2)}) %copy-start.1) | copy-done | bytes 536
  1.4 0.0 copy-start
  1.4 0.2 copy.25
  1.6 0.5 copy-done
  2.1 0.2 copy.21
  2.2 0.1 fusion
  2.4 0.8 %fusion.12.meta_ref = bf16[2,8,16,64]{3,2,1,0:T(8,128)(2,1)} fusion(bf16[2,8,16,1]{3,2,1,0:T(8,128)(2,1)S(1)} %fusion.8, bf16[2,8,16,1]{3,2,1,0:T(8,128)(2,1)S(1)} %copy.25, bf16[2,8,16,1]{3,2,1,0:T(8,128)(2,1)S(1)} %get-tuple-element.6, bf16[2,8,16,1]{3,2,1,0:T(8,128)(2,1)S(1)} %get-tuple-element.5), kind=kLoop, calls=%fused_computation.20 | loop fusion | flops 212992 | bytes 34816 | tf_op jit(solution)/shard_map/stack | solution.py:285
  3.1 46.3 %shard_map.109 = bf16[32,32,192]{2,1,0:T(8,128)(2,1)} custom-call(bf16[32,32,192]{2,1,0:T(8,128)(2,1)} %bitcast.12, bf16[2,32,32,192]{3,2,1,0:T(8,128)(2,1)} %bitcast.11, f32[7,7,192]{2,1,0:T(8,128)} %kern_hbm.1, f32[1,192]{1,0:T(1,128)} %bitcast.19, bf16[192,768]{1,0:T(8,128)(2,1)} %up_hbm.1, f32[6,128]{1,0:T(8,128)} %bitcast.16, ...), custom_call_target="tpu_custom_call" | custom-call | tf_op jit(solution)/shard_map/pallas_call | solution.py:294
  49.4 1.9 %copy.27 = bf16[1,32,32,192]{3,2,1,0:T(8,128)(2,1)} copy(bf16[1,32,32,192]{3,2,1,0:T(8,128)(2,1)} %bitcast.10) | data formatting | bytes 786432
Async XLA Ops:
  0.0 0.7 %copy-start.2 = (s32[2,1,8]{2,1,0:T(1,128)S(1)}, s32[2,1,8]{2,1,0:T(1,128)}, u32[]{:S(2)}) copy-start(s32[2,1,8]{2,1,0:T(1,128)} %param.19) | copy-start | bytes 196
  0.7 0.7 %copy-start.1 = (bf16[2,1,8,16]{3,2,1,0:T(8,128)(2,1)S(1)}, bf16[2,1,8,16]{3,2,1,0:T(8,128)(2,1)}, u32[]{:S(2)}) copy-start(bf16[2,1,8,16]{3,2,1,0:T(8,128)(2,1)} %param.21) | copy-start | bytes 1540
  1.4 0.7 %copy-start = (s32[2,1,8,16]{3,2,1,0:T(8,128)S(1)}, s32[2,1,8,16]{3,2,1,0:T(8,128)}, u32[]{:S(2)}) copy-start(s32[2,1,8,16]{3,2,1,0:T(8,128)} %param.18) | copy-start | bytes 3076

commit v3 on v2

--- a/solution.py
+++ b/solution.py
@@ -14,7 +14,6 @@
 MESH = pl.DeviceIdType.MESH
 F32, BF16 = jnp.float32, jnp.bfloat16
 GROUP = 4
-PAD = 8
 
 
 def gelu_slope(u):
@@ -25,9 +24,8 @@
 
 
 def kernel(
-    tiles, members, adj_hbm, st_hbm, kern_hbm, gain_hbm, up_hbm, bias_hbm, down_hbm, obs_hbm, meta_ref, out_ref,
-    adj_ref, st_ref, kern_ref, gain_ref, up_ref, bias_ref, downt, obs_ref, pack_ref,
-    xb, ahb, cur, plane0, plane1, kbr, hbuf, turn, upt, orecv, samp, dep, local_sem,
+    tiles, members, adj_ref, st_ref, kern_ref, gain_ref, up_ref, bias_ref, downt, obs_ref, meta_ref, out_ref,
+    pack_ref, xb, ahb, cur, plane1, kbr, hbuf, turn, upt, orecv, samp, dep,
     obs_send, obs_recv, mem_send, mem_recv, halo_send, halo_recv,
 ):
     steps, lat, lon, chan = st_ref.shape
@@ -36,15 +34,6 @@
     pitch = turn.shape[1] // lon
     rows = GROUP * lat
     t, m = lax.axis_index("tile"), lax.axis_index("member")
-
-    loads = []
-    for src, dst in (
-        (obs_hbm, obs_ref), *((st_hbm.at[s], st_ref.at[s]) for s in range(steps)), (kern_hbm, kern_ref),
-        (up_hbm, up_ref), (adj_hbm, adj_ref), (down_hbm, downt), (gain_hbm, gain_ref), (bias_hbm, bias_ref),
-    ):
-        loads.append(pltpu.make_async_copy(src, dst, local_sem.at[len(loads)]))
-        loads[-1].start()
-    obs_load, st_loads, other_loads = loads[0], loads[1:1 + steps], loads[1 + steps:]
 
     barrier = pltpu.get_barrier_semaphore()
     for d in range(1, tiles):
@@ -76,10 +65,8 @@
         def store_x(k, a, b):
             xb[s, 3 + k, :, :128] = a.astype(BF16)
             xb[s, 3 + k, :, 128:] = b.astype(BF16)
-        st_loads[s].wait()
         to_lon_major(lambda i: st_ref[s, i], store_x)
 
-    obs_load.wait()
     for s in range(steps):
         pack_ref[:, s, :, :chan] = obs_ref[s]
         pack_ref[:, s, :, chan:] = meta_ref[s]
@@ -100,8 +87,6 @@
             turn_state(s)
         for c in halos[s]:
             c.start()
-    for c in other_loads:
-        c.wait()
 
     def store_adj(k, a, b):
         cur[k, :, :128] = a.astype(BF16)
@@ -110,14 +95,10 @@
     upt[...] = up_ref[...].T
     for n in range(49):
         taps = kern_ref[n // 7, n % 7:n % 7 + 1, :]
-        kbr[0, n] = jnp.broadcast_to(taps[:, :128], (8, 128))
-        tail = jnp.broadcast_to(taps[:, 128:], (8, rest))
+        kbr[0, n] = jnp.broadcast_to(taps[:, :128], (16, 128)).astype(BF16)
+        tail = jnp.broadcast_to(taps[:, 128:], (16, rest)).astype(BF16)
         kbr[1, n, :, :rest] = tail
         kbr[1, n, :, rest:] = tail
-    for plane in (plane0, plane1):
-        plane[:, :PAD] = jnp.zeros((plane.shape[0], PAD, 128), F32)
-        plane[:, PAD + lat:] = jnp.zeros((plane.shape[0], PAD, 128), F32)
-
     for c in obs:
         c.wait()
 
@@ -141,39 +122,37 @@
             mem[s][-1].start()
 
     def build(buf, s, wait):
-        def put0(i, _):
-            plane0[i, PAD:PAD + lat, :] = buf[s, i, :, :128].astype(F32)
+        def put1(i, _):
+            plane1[i] = jnp.concatenate(
+                [buf[s, i, :, 128:].astype(F32), buf[s, i + half, :, 128:].astype(F32)], axis=-1).astype(BF16)
             return 0
-
-        def put1(i, _):
-            plane1[i, PAD:PAD + lat, :] = jnp.concatenate(
-                [buf[s, i, :, 128:].astype(F32), buf[s, i + half, :, 128:].astype(F32)], axis=-1)
-            return 0
-        lax.fori_loop(3, lon + 3, put0, 0)
         lax.fori_loop(3, half + 3, put1, 0)
         wait()
-        for lo in (0, lon + 3):
-            lax.fori_loop(lo, lo + 3, put0, 0)
         for lo in (0, half + 3):
             lax.fori_loop(lo, lo + 3, put1, 0)
 
-    def conv_group(plane, p_id, first, flip):
+    def conv_group(load, p_id, flip):
+        views = [load(r).reshape(lat // 16, 16, 128) for r in range(GROUP + 6)]
+        line_at = lax.broadcasted_iota(jnp.int32, (lat, 128), 0)
         acc = [None] * GROUP
         for p in range(7):
-            for r in range(GROUP + 6):
-                v = plane[first + r, pl.ds(PAD - 3 + p, lat), :].reshape(lat // 8, 8, 128)
-                for q in range(7):
-                    o = r - q
-                    if 0 <= o < GROUP:
-                        n = (6 - p) * 7 + (6 - q) if flip else p * 7 + q
-                        term = kbr[p_id, n][None] * v
-                        acc[o] = term if acc[o] is None else acc[o] + term
-        return jnp.concatenate([a.reshape(lat, 128) for a in acc], axis=0)
-
-    def conv(i0, flip, to):
-        hbuf[to, :rows, :128] = conv_group(plane0, 0, i0, flip)
-        hbuf[to, rows:, :128] = conv_group(plane0, 0, half + i0, flip)
-        both = conv_group(plane1, 1, i0, flip)
+            shift = p - 3
+            taps = [kbr[p_id, (6 - p) * 7 + (6 - q) if flip else p * 7 + q][None] for q in range(7)]
+            for o in range(GROUP):
+                t = [taps[q] * views[o + q] for q in range(7)]
+                part = ((t[0] + t[1]) + (t[2] + t[3])) + ((t[4] + t[5]) + t[6])
+                part = part.reshape(lat, 128).astype(F32)
+                if shift:
+                    part = pltpu.roll(part, (-shift) % lat, 0)
+                    inside = line_at < lat - shift if shift > 0 else line_at >= -shift
+                    part = jnp.where(inside, part, 0.0)
+                acc[o] = part if acc[o] is None else acc[o] + part
+        return jnp.concatenate(acc, axis=0)
+
+    def conv(buf, s, i0, flip, to):
+        hbuf[to, :rows, :128] = conv_group(lambda r: buf[s, i0 + r, :, :128], 0, flip)
+        hbuf[to, rows:, :128] = conv_group(lambda r: buf[s, half + i0 + r, :, :128], 0, flip)
+        both = conv_group(lambda r: plane1[i0 + r], 1, flip)
         hbuf[to, :rows, 128:] = both[:, :rest]
         hbuf[to, rows:, 128:] = both[:, rest:]
 
@@ -210,19 +189,16 @@
             ahb[s, pl.ds(3 + i0, GROUP)] = ah[:rows].reshape(GROUP, lat, chan)
             ahb[s, pl.ds(3 + half + i0, GROUP)] = ah[rows:].reshape(GROUP, lat, chan)
 
-        def both_parts(k, _, back=back, point=point):
-            hidden = hbuf[lax.rem(k, 2)]
-            conv(at_turn(k + 1), False, lax.rem(k + 1, 2))
-            point(k, hidden)
+        def both_parts(k, _, s=s, back=back, point=point):
+            conv(xb, s, at_turn(k), False, 0)
+            point(k, hbuf[0])
 
             @pl.when(k == 1)
             def _():
                 for c in back:
                     c.start()
             return 0
-        conv(at_turn(0), False, 0)
-        lax.fori_loop(0, blocks - 1, both_parts, 0)
-        point(blocks - 1, hbuf[(blocks - 1) % 2])
+        lax.fori_loop(0, blocks, both_parts, 0)
 
         for c in mem[s]:
             c.wait()
@@ -247,7 +223,7 @@
 
         def spread(k, _, s=s, line=line):
             i0 = k * GROUP
-            conv(i0, True, 0)
+            conv(ahb, s, i0, True, 0)
             back_out = hbuf[0]
             row = lax.broadcasted_iota(jnp.int32, (2 * rows, slots), 0)
             row = jnp.where(row < rows, row, row + (half * lat - rows)) + i0 * lat
@@ -294,31 +270,21 @@
     out = pl.pallas_call(
         functools.partial(kernel, tiles, members),
         out_shape=jax.ShapeDtypeStruct((lat, lon, chan), BF16),
-        in_specs=[pl.BlockSpec(memory_space=pltpu.HBM)] * 8 + [vm],
+        in_specs=[vm] * 9,
         out_specs=vm,
         scratch_shapes=[
-            pltpu.VMEM((lat, lon, chan), BF16),
-            pltpu.VMEM((steps, lat, lon, chan), BF16),
-            pltpu.VMEM((7, 7, chan), F32),
-            pltpu.VMEM((1, chan), F32),
-            pltpu.VMEM((chan, hid), BF16),
-            pltpu.VMEM((hid // 128, 128), F32),
-            pltpu.VMEM((chan, hid), BF16),
-            pltpu.VMEM((steps, tiles, cap, chan), BF16),
             pltpu.VMEM((tiles, steps, cap, 256), BF16),
             pltpu.VMEM((steps, lon + 6, lat, chan), BF16),
             pltpu.VMEM((steps, lon + 6, lat, chan), BF16),
             pltpu.VMEM((lon, lat, chan), BF16),
-            pltpu.VMEM((lon + 6, lat + 2 * PAD, 128), F32),
-            pltpu.VMEM((lon // 2 + 6, lat + 2 * PAD, 128), F32),
-            pltpu.VMEM((2, 49, 8, 128), F32),
-            pltpu.VMEM((2, 2 * GROUP * lat, chan), F32),
+            pltpu.VMEM((lon // 2 + 6, lat, 128), BF16),
+            pltpu.VMEM((2, 49, 16, 128), BF16),
+            pltpu.VMEM((1, 2 * GROUP * lat, chan), F32),
             pltpu.VMEM((2, pitch * lon, 128), F32),
             pltpu.VMEM((hid, chan), BF16),
             pltpu.VMEM((tiles, steps, cap, 256), BF16),
             pltpu.VMEM((members, steps, slots, chan), BF16),
             pltpu.VMEM((steps, slots, chan), BF16),
-            pltpu.SemaphoreType.DMA((steps + 7,)),
             pltpu.SemaphoreType.DMA((tiles,)),
             pltpu.SemaphoreType.DMA((tiles,)),
             pltpu.SemaphoreType.DMA((steps, members)),
@@ -327,7 +293,7 @@
             pltpu.SemaphoreType.DMA((2 * steps, 2)),
         ],
         compiler_params=pltpu.CompilerParams(
-            collective_id=0, has_side_effects=True, vmem_limit_bytes=127 * 512 * 1024),
+            collective_id=0, has_side_effects=True, vmem_limit_bytes=48 * 1024 * 1024),
     )(
         adjoint_final[0], states[:, 0], kernel_w, norm_gain.reshape(1, chan),
         up_weight, up_bias.reshape(hid // 128, 128), down_weight.T, obs_value[:, 0], meta,

time: 51.6 us -> 46.2 us (0.90)
  Pallas kernels: 46.3 us -> 38.4 us
  local copies, waits for them, and re-layouts: 4.01 us -> 6.3 us
    pallas_call x1, Pallas kernels: 46.3 us -> 38.4 us  [per_device(): pl.pallas_call(functools.partial(kernel, tiles, members), out_shape=jax.S...]
    unnamed x7 -> x17, local copies, waits for them, and re-layouts: 3.65 us -> 4.57 us
    convert_element_type x1, other arithmetic: 0.08 us -> 0.82 us  [per_device(): (slot < obs_count[:, 0][..., None]).astype(BF16)]
    squeeze x1, local copies, waits for them, and re-layouts: 0.17 us -> 0.86 us  [per_device(): cell = obs_cell[:, 0]]
    another operation x1, local copies, waits for them, and re-layouts: 0.19 us -> 0.87 us  [per_device(): jnp.stack([(cell % lon).astype(BF16), (cell // lon + lax.axis_index('tile...]
    another operation x1, other arithmetic: 0.76 us -> 0.13 us  [per_device(): jnp.stack([(cell % lon).astype(BF16), (cell // lon + lax.axis_index('tile...]
where the time goes in v3:
time: 46.2 us; the launch traced here: 45.9 us
  Pallas kernels  38.4 us (83%)
  local copies, waits for them, and re-layouts  6.3 us (14%)
  other arithmetic  1.09 us (2%)
    pallas_call x1, Pallas kernels, per_device(): pl.pallas_call(functools.partial(kernel, tiles, members), out_shape=jax.S...  38.4 us
    unnamed x17, local copies, waits for them, and re-layouts  4.57 us

profile of v3, /device:TPU:1, one launch (start us, length us, event | category | flops | bytes accessed | tf_op | source)
XLA Modules:
  0.0 45.9 jit_solution(6063020678075750644)
XLA Ops:
  0.0 0.0 copy-start.1
  0.0 0.8 %fusion.8 = bf16[2,8,16,1]{3,2,1,0:T(8,128)(2,1)S(1)} fusion(s32[2,8]{1,0:T(2,128)} %bitcast.19), kind=kLoop, calls=%fused_computation.16 | loop fusion | flops 512 | bytes 576 | tf_op jit(solution)/shard_map/convert_element_type | solution.py:265
  0.8 0.9 %copy.25 = bf16[2,8,16,1]{3,2,1,0:T(8,128)(2,1)S(1)} copy(bf16[2,8,16,1]{2,1,0,3:T(8,128)(2,1)} %bitcast.18) | data formatting | bytes 1024 | tf_op jit(solution)/shard_map/stack;squeeze | solution.py:261
  1.7 0.9 %copy.21 = s32[2,8,16,1]{3,2,1,0:T(8,128)S(1)} copy(s32[2,8,16,1]{2,1,0,3:T(8,128)} %bitcast.17) | data formatting | bytes 2048 | tf_op jit(solution)/shard_map/squeeze | solution.py:259
  2.6 0.0 copy-start.2
  2.6 0.1 fusion
  2.7 0.0 copy-start.5
  2.7 0.0 copy-start.6
  2.7 0.0 copy-start.7
  2.7 0.1 fusion.12.meta_ref
  2.9 0.0 copy-done.1
  2.9 0.6 %copy-done.2 = bf16[192,768]{1,0:T(8,128)(2,1)S(1)} copy-done((bf16[192,768]{1,0:T(8,128)(2,1)S(1)}, bf16[192,768]{1,0:T(8,128)(2,1)}, u32[]{:S(2)}) %copy-start.2) | copy-done | bytes 294936
  3.5 0.0 copy-done.5
  3.5 0.0 copy-done.6
  3.6 0.0 copy-done.7
  3.6 0.0 copy-start
  3.6 1.2 %copy-done = bf16[2,1,32,32,192]{4,3,2,1,0:T(8,128)(2,1)S(1)} copy-done((bf16[2,1,32,32,192]{4,3,2,1,0:T(8,128)(2,1)S(1)}, bf16[2,1,32,32,192]{4,3,2,1,0:T(8,128)(2,1)}, u32[]{:S(2)}) %copy-start) | copy-done | bytes 786456
  4.8 0.0 copy-start.3
  4.8 1.0 %copy-done.3 = bf16[768,192]{0,1:T(8,128)(2,1)S(1)} copy-done((bf16[768,192]{0,1:T(8,128)(2,1)S(1)}, bf16[768,192]{0,1:T(8,128)(2,1)}, u32[]{:S(2)}) %copy-start.3) | copy-done | bytes 294936
  5.7 0.0 copy-start.4
  5.7 0.9 %copy-done.4 = bf16[2,1,8,16,192]{4,3,2,1,0:T(8,128)(2,1)S(1)} copy-done((bf16[2,1,8,16,192]{4,3,2,1,0:T(8,128)(2,1)S(1)}, bf16[2,1,8,16,192]{4,3,2,1,0:T(8,128)(2,1)}, u32[]{:S(2)}) %copy-start.4) | copy-done | bytes 98328
  6.6 38.4 %shard_map.109 = bf16[32,32,192]{2,1,0:T(8,128)(2,1)S(1)} custom-call(bf16[32,32,192]{2,1,0:T(8,128)(2,1)S(1)} %bitcast.12, bf16[2,32,32,192]{3,2,1,0:T(8,128)(2,1)S(1)} %bitcast.11, f32[7,7,192]{2,1,0:T(8,128)S(1)} %copy-done.5, f32[1,192]{1,0:T(1,128)S(1)} %bitcast.16, bf16[192,768]{1,0:T(8,128)(2,1)S(1)} %copy-done.2, f32[6,128]{1,0:T(8,128)S(1)} %bitcast.15, ...), custom_call_target="tpu_custom_call" | custom-call | tf_op jit(solution)/shard_map/pallas_call | solution.py:270
  45.1 0.8 %copy.27 = bf16[1,32,32,192]{3,2,1,0:T(8,128)(2,1)} copy(bf16[1,32,32,192]{3,2,1,0:T(8,128)(2,1)S(1)} %bitcast.10) | data formatting | bytes 786432
Async XLA Ops:
  0.0 2.9 %copy-start.1 = (bf16[1,32,32,192]{3,2,1,0:T(8,128)(2,1)S(1)}, bf16[1,32,32,192]{3,2,1,0:T(8,128)(2,1)}, u32[]{:S(2)}) copy-start(bf16[1,32,32,192]{3,2,1,0:T(8,128)(2,1)} %param.11) | copy-start | bytes 1179652
  2.6 1.0 %copy-start.2 = (bf16[192,768]{1,0:T(8,128)(2,1)S(1)}, bf16[192,768]{1,0:T(8,128)(2,1)}, u32[]{:S(2)}) copy-start(bf16[192,768]{1,0:T(8,128)(2,1)} %up_ref.1) | copy-start | bytes 884740
  2.7 0.8 %copy-start.5 = (f32[7,7,192]{2,1,0:T(8,128)S(1)}, f32[7,7,192]{2,1,0:T(8,128)}, u32[]{:S(2)}) copy-start(f32[7,7,192]{2,1,0:T(8,128)} %kern_ref.1) | copy-start | bytes 112900
  2.7 0.8 %copy-start.6 = (f32[768]{0:T(1024)S(1)}, f32[768]{0:T(1024)}, u32[]{:S(2)}) copy-start(f32[768]{0:T(1024)} %param.16) | copy-start | bytes 9220
  2.7 0.8 %copy-start.7 = (f32[192]{0:T(256)S(1)}, f32[192]{0:T(256)}, u32[]{:S(2)}) copy-start(f32[192]{0:T(256)} %param.14) | copy-start | bytes 2308
  3.6 1.2 %copy-start = (bf16[2,1,32,32,192]{4,3,2,1,0:T(8,128)(2,1)S(1)}, bf16[2,1,32,32,192]{4,3,2,1,0:T(8,128)(2,1)}, u32[]{:S(2)}) copy-start(bf16[2,1,32,32,192]{4,3,2,1,0:T(8,128)(2,1)} %param.12) | copy-start | bytes 2359300
  4.8 1.0 %copy-start.3 = (bf16[768,192]{0,1:T(8,128)(2,1)S(1)}, bf16[768,192]{0,1:T(8,128)(2,1)}, u32[]{:S(2)}) copy-start(bf16[768,192]{0,1:T(8,128)(2,1)} %param.17) | copy-start | bytes 884740
  5.7 0.9 %copy-start.4 = (bf16[2,1,8,16,192]{4,3,2,1,0:T(8,128)(2,1)S(1)}, bf16[2,1,8,16,192]{4,3,2,1,0:T(8,128)(2,1)}, u32[]{:S(2)}) copy-start(bf16[2,1,8,16,192]{4,3,2,1,0:T(8,128)(2,1)} %param.20) | copy-start | bytes 294916
